TPU v7x, 512 devices: a whole 4x4x16 slice. The times are simulated.
512 devices in a mesh: seq: 64 (over z, x_hi, core), grp: 8 (over x_lo, y).
Axes of the slice: x: 4 (x_hi: 2, x_lo: 2; x = x_hi * 2 + x_lo), y: 4, z: 16, core: 2. Of those that a mesh axis runs over, the one named last changes fastest.
Arguments:
- inputs: bfloat16 [65536, 2048], P('seq', 'grp'), may hold values from -6 to 6
- out_grad: bfloat16 [65536, 2048], P('seq', 'grp'), may hold values from -6 to 6
- filt: bfloat16 [128, 2048], P('grp'), may hold values from -0.125 to 0.125
- band: int32 [128, 16], P('grp'), may hold values from 0 to 1, as said below
Outputs:
- input_grad: bfloat16 [65536, 2048], P(('seq', 'grp'))
- filter_grad: float32 [128, 2048], P('grp', 'seq')
Inputs may be any that keep to these rules, and one draw needn't show every extreme that they name: Each row of band is a truncation: ones at offsets 0 .. L - 1 and zeros after, with 1 <= L <= 16; some group keeps all 16 offsets.
All inputs are finite; a program needn't handle non-finite values.
Results may differ from a plain program's by a relative error of at most 0.001.
Values may be sent and summed in bfloat16 or wider, within the bound.
No kernel may reach another device: no remote copies, remote signals or barrier semaphores. Data moves between devices by JAX's collectives and lax.ppermute only.
A program may use at most 64 MiB of HBM per device.

v0:
```python
import math

import jax
import jax.numpy as jnp
from jax import lax
from jax.sharding import PartitionSpec as P

CPG = 16
BLK = 128
NOFF = 16


def from_behind(block, axis, distance):
    devices = range(lax.axis_size(axis))
    route = [(i - distance, i) for i in devices if i - distance in devices]
    return lax.ppermute(block, axis, route)


def build_tile(filt_pad, keep, offset, width_blk):
    window = lax.dynamic_slice_in_dim(filt_pad, offset * width_blk, 2 * width_blk, 1)
    groups_here = window.shape[0]
    turned = jnp.roll(window[:, ::-1], -(width_blk - 1), axis=1)
    repeated = jnp.tile(turned, (1, width_blk))[:, : width_blk * (2 * width_blk - 1)]
    tile = repeated.reshape(groups_here, width_blk, 2 * width_blk - 1)[:, :, :width_blk]
    return jnp.where((keep > 0)[:, None, None], tile, jnp.zeros_like(tile))


def flip_pad(blocks):
    return jnp.concatenate([blocks[:, ::-1], jnp.zeros_like(blocks)], axis=1)


def diagonal_sums(product):
    groups_here = product.shape[0]
    width_blk = product.shape[1]
    flat = product.reshape(groups_here, 2 * width_blk * width_blk)[
        :, : width_blk * (2 * width_blk - 1)
    ]
    return jnp.sum(flat.reshape(groups_here, width_blk, 2 * width_blk - 1), axis=1)


def per_device(inputs, out_grad, filt, band):
    tok_rows, channels = inputs.shape
    block_count = tok_rows // BLK
    groups_here = channels // CPG
    reach_devs = (NOFF + block_count - 2) // block_count
    own_grad = out_grad.reshape(block_count, BLK, groups_here, CPG)
    filt_pad = jnp.concatenate([jnp.zeros((groups_here, BLK), jnp.bfloat16), filt], axis=1)
    later_list = [out_grad]
    moving = out_grad
    for stride in range(reach_devs):
        moving = from_behind(moving, "seq", -1)
        later_list.append(moving)
    grad_window = jnp.concatenate(later_list, axis=0).reshape(-1, BLK, groups_here, CPG)
    earlier_list = [inputs]
    moving_in = inputs
    for stride in range(reach_devs):
        moving_in = from_behind(moving_in, "seq", 1)
        earlier_list.insert(0, moving_in)
    padded_window = flip_pad(
        jnp.concatenate(earlier_list, axis=0).reshape(-1, BLK, groups_here, CPG)
    )

    def offset_step(offset, carry):
        keep = lax.dynamic_index_in_dim(band, offset, 1, keepdims=False)
        dx_acc, dh_acc = carry
        tile = build_tile(filt_pad, keep, offset, BLK)
        later = lax.dynamic_slice_in_dim(grad_window, offset, block_count, 0)
        dx_acc = dx_acc + jnp.einsum(
            "gab,jagc->jbgc", tile, later, preferred_element_type=jnp.float32
        )
        earlier = lax.dynamic_slice_in_dim(
            padded_window, reach_devs * block_count - offset, block_count, 0
        )
        product = jnp.einsum(
            "jagc,jbgc->gab", own_grad, earlier, preferred_element_type=jnp.float32
        )
        sums = diagonal_sums(product) * (keep > 0).astype(jnp.float32)[:, None]
        start = offset * BLK + 1
        current = lax.dynamic_slice_in_dim(dh_acc, start, 2 * BLK - 1, 1)
        dh_acc = lax.dynamic_update_slice_in_dim(dh_acc, current + sums, start, 1)
        return (dx_acc, dh_acc)

    init = (
        jnp.zeros((block_count, BLK, groups_here, CPG), jnp.float32),
        jnp.zeros((groups_here, NOFF * BLK + BLK), jnp.float32),
    )
    dx_acc, dh_acc = lax.fori_loop(0, NOFF, offset_step, init)
    total_rows = tok_rows * lax.axis_size("seq")
    scale = 1.0 / math.sqrt(total_rows * CPG)
    partial_grad = dh_acc[:, BLK:] * scale
    filter_grad = lax.psum_scatter(partial_grad, "seq", scatter_dimension=1, tiled=True)
    input_local = dx_acc.reshape(tok_rows, channels).astype(jnp.bfloat16)
    input_grad = lax.all_to_all(input_local, "grp", split_axis=0, concat_axis=1, tiled=True)
    return (input_grad, filter_grad)


def solution(mesh):
    return jax.shard_map(
        per_device,
        mesh=mesh,
        in_specs=(P("seq", "grp"), P("seq", "grp"), P("grp", None), P("grp", None)),
        out_specs=(P(("seq", "grp"), None), P("grp", "seq")),
        check_vma=False,
    )
```

profile of v0, /device:TPU:8, one launch (start us, length us, event | category | flops | bytes accessed | tf_op | source)
XLA Modules:
  0.0 639.2 jit_solution(8245572267647411322)
XLA Ops:
  10.8 15.6 %collective-permute-start.3 = (bf16[1024,256]{1,0:T(8,128)(2,1)S(1)}, bf16[1024,256]{1,0:T(8,128)(2,1)S(1)}, u32[]{:S(2)}, u32[]{:S(2)}) collective-permute-start(bf16[1024,256]{1,0:T(8,128)(2,1)S(1)} %collective-permute-done.2), channel_id=1, source_target_pairs={{0,8},{8,16},{16,24},{24,32},{32,40},{40,48},{48,56},{56,64},{64,7... | collective-permute-start | bytes 1572872 | tf_op jit(solution)/shard_map/ppermute | solution.py:16
  33.2 4.5 rev.6
  46.0 344.3 %while.18 = (s32[]{:T(128)}, f32[8,128,16,16]{1,3,0,2:T(8,128)}, f32[16,2176]{1,0:T(8,128)S(1)}, bf16[24,128,16,16]{1,0,3,2:T(8,128)(2,1)}, s32[16,16]{0,1:T(8,1...) while((s32[]{:T(128)}, f32[8,128,16,16]{1,3,0,2:T(8,128)}, ...), condition=%wide.region_2.3_spmd.clone, body=%wide.region_0.2_spmd.clone.sunk | while | flops 202655760 | bytes 32096948 | solution.py:87
  60.6 4.8 reshape.78
  82.2 4.8 reshape.78
  103.8 4.8 reshape.78
  112.0 3.4 reshape.77
  125.5 4.8 reshape.78
  147.1 4.8 reshape.78
  155.3 3.4 reshape.77
  168.7 4.8 reshape.78
  190.3 4.8 reshape.78
  212.0 4.8 reshape.78
  233.6 4.8 reshape.78
  241.8 3.4 reshape.77
  255.2 4.8 reshape.78
  276.9 4.8 reshape.78
  298.5 4.8 reshape.78
  320.1 4.8 reshape.78
  341.7 4.8 reshape.78
  363.4 4.8 reshape.78
  385.0 4.8 reshape.78
  392.5 4.9 all-to-all-start
  398.7 231.3 %reduce-scatter.4.cloned.1.call-done = f32[32,16]{1,0:T(8,128)} async-done(((f32[2048,16]{1,0:T(8,128)}), f32[32,16]{1,0:T(8,128)}) %reduce-scatter.4.cloned.1.call-update) | async-done | bytes 2064
  (352 shorter events, 279.7 us)
Async XLA Ops:
  7.2 23.6 %copy-start.1 = (bf16[1024,256]{1,0:T(8,128)(2,1)S(1)}, bf16[1024,256]{1,0:T(8,128)(2,1)}, u32[]{:S(2)}) copy-start(bf16[1024,256]{1,0:T(8,128)(2,1)} %param.6) | copy-start | bytes 1572868
  7.2 23.5 %copy-start.2 = (bf16[16,2048]{1,0:T(8,128)(2,1)S(1)}, bf16[16,2048]{1,0:T(8,128)(2,1)}, u32[]{:S(2)}) copy-start(bf16[16,2048]{1,0:T(8,128)(2,1)} %param.8) | copy-start | bytes 196612
  7.2 3.6 collective-permute-start.2
  9.1 17.3 %collective-permute-start = (bf16[1024,256]{1,0:T(8,128)(2,1)}, bf16[1024,256]{1,0:T(8,128)(2,1)}, u32[]{:S(2)}, u32[]{:S(2)}) collective-permute-start(bf16[1024,256]{1,0:T(8,128)(2,1)} %param.7), channel_id=1, source_target_pairs={{8,0},{16,8},{24,16},{32,24},{40,32},{48,40},{56,48},{64,56},{72,6... | collective-permute-start | bytes 1572872 | tf_op jit(solution)/shard_map/ppermute | solution.py:16
  10.8 19.9 %collective-permute-start.3 = (bf16[1024,256]{1,0:T(8,128)(2,1)S(1)}, bf16[1024,256]{1,0:T(8,128)(2,1)S(1)}, u32[]{:S(2)}, u32[]{:S(2)}) collective-permute-start(bf16[1024,256]{1,0:T(8,128)(2,1)S(1)} %collective-permute-done.2), channel_id=1, source_target_pairs={{0,8},{8,16},{16,24},{24,32},{32,40},{40,48},{48,56},{56,64},{64,7... | collective-permute-start | bytes 1572872 | tf_op jit(solution)/shard_map/ppermute | solution.py:16
  26.4 11.4 %collective-permute-start.1 = (bf16[1024,256]{1,0:T(8,128)(2,1)}, bf16[1024,256]{1,0:T(8,128)(2,1)}, u32[]{:S(2)}, u32[]{:S(2)}) collective-permute-start(bf16[1024,256]{1,0:T(8,128)(2,1)} %collective-permute-done), channel_id=1, source_target_pairs={{8,0},{16,8},{24,16},{32,24},{40,32},{48,40},{56,48},{64,56},{72,6... | collective-permute-start | bytes 1572872 | tf_op jit(solution)/shard_map/ppermute | solution.py:16
  43.9 2.1 copy-start
  392.5 238.9 %all-to-all-start = ((bf16[8,128,256]{1,2,0:T(8,128)(2,1)}), bf16[8,128,256]{1,2,0:T(8,128)(2,1)S(1)}, u32[]{:S(2)}, u32[]{:S(2)}) async-start(bf16[8,128,256]{1,2,0:T(8,128)(2,1)} %bitcast), calls=%async_computation | async-start | bytes 1048576 | tf_op jit(solution)/shard_map/all_to_all | solution.py:93
  397.4 232.6 %reduce-scatter.4.cloned.1.call-start = ((), (), s32[]{:S(2)}) async-start(), calls=%async_computation.2 | async-start | bytes 1064960
Sparse Core Ops, SparseCore 0:
  402.8 227.1 reduce-scatter.3
where the time goes:
time: 642 us; the launch traced here: 639 us
  local copies, waits for them, and re-layouts  290 us (45%)
  waiting for transfers between devices  232 us (36%)
  matrix products  69.4 us (11%)
  starting transfers between devices  25 us (4%)
  between operations  14.2 us (2%)
  other arithmetic  7.06 us (1%)
    unnamed x2, waiting for transfers between devices  231 us
    reshape x16, local copies, waits for them, and re-layouts, diagonal_sums(): flat.reshape(groups_here, width_blk, 2 * width_blk - 1)  77 us
    reshape x16, local copies, waits for them, and re-layouts, build_tile(): repeated.reshape(groups_here, width_blk, 2 * width_blk - 1)  53.7 us
    while x64, local copies, waits for them, and re-layouts  48.5 us
    dot_general x16, matrix products, offset_step(): jnp.einsum('gab,jagc->jbgc', tile, later, preferred_element_type=jnp.floa...  40.2 us
    dynamic_slice x16, local copies, waits for them, and re-layouts, offset_step(): lax.dynamic_slice_in_dim(padded_window, reach_devs * block_count - offset...  30.7 us
    dot_general x16, matrix products, offset_step(): jnp.einsum('jagc,jbgc->gab', own_grad, earlier, preferred_element_type=jn...  29.3 us
    slice x16, local copies, waits for them, and re-layouts, diagonal_sums(): product.reshape(groups_here, 2 * width_blk * width_blk)  23.7 us
  transfers between devices with their start and end apart: 6, of which 2 were waited for; matrix products, arithmetic and copies ran while one was open for 2% of the time, Pallas kernels for 0%

commit v1 on v0

v1 whole, which is shorter than its diff:
```python
import functools
import math

import jax
import jax.numpy as jnp
from jax import lax
from jax.experimental import pallas as pl
from jax.experimental.pallas import tpu as pltpu
from jax.sharding import Mesh
from jax.sharding import PartitionSpec as P

CPG = 16
BLK = 128
NOFF = 16
LANES = 128
QUART = 32
BF16 = jnp.bfloat16
F32 = jnp.float32
VMEM = pl.BlockSpec(memory_space=pltpu.VMEM)
SMEM = pl.BlockSpec(memory_space=pltpu.SMEM)
PARAMS = pltpu.CompilerParams(vmem_limit_bytes=48 << 20)


def aligned(start, size):
    return pl.ds(pl.multiple_of(start, size), size)


def tiles_kernel(level, turned_filt, tile_ref):
    row = lax.broadcasted_iota(jnp.int32, (BLK, BLK), 0)
    col = lax.broadcasted_iota(jnp.int32, (BLK, BLK), 1)

    def one_group(g, _):
        lags = turned_filt[g]
        before = jnp.zeros((BLK, BLK), F32)
        for k in range(NOFF):
            spread = jnp.broadcast_to(lags[k : k + 1], (BLK, BLK))
            here = pltpu.roll(spread, 1, 1, stride=1, stride_axis=0)
            tile = jnp.where(col > row, before, here)
            tile = jnp.where(k < level[g], tile, 0.0)
            tile_ref[g, k * BLK : (k + 1) * BLK, :] = tile.astype(BF16)
            before = here
        return 0

    lax.fori_loop(0, turned_filt.shape[0], one_group, 0)


def main_kernel(
    level, core, tile_ref, dy_own, x_own, pair, later_same, later_other, dx_ref, send_ref, dy_t, x_t, dh_ref
):
    groups = tile_ref.shape[0]
    per_core = dy_own.shape[0] // BLK
    blocks = 2 * per_core
    h = core[0]

    def turn(src, first, lane, i):
        block = src[aligned((first + i) * BLK, BLK), lane]
        return block.T.reshape(groups, CPG, BLK)

    def put_dy(src, base, lane=slice(None)):
        for i in range(per_core):
            turned = turn(src, 0, lane, i)
            at = (base + i) * CPG
            dy_t[:, aligned(at + CPG, CPG), :BLK] = turned
            dy_t[:, aligned(at, CPG), BLK:] = turned

    def put_x(src, first, base, lane=slice(None)):
        for i in range(per_core):
            x_t[:, aligned((base + i) * CPG, CPG), :] = turn(src, first, lane, i)

    mine = aligned(h * LANES, LANES)
    put_dy(dy_own, h * per_core, mine)
    put_dy(pair, (1 - h) * per_core)
    put_dy(later_same, blocks + h * per_core)
    put_dy(later_other, blocks + (1 - h) * per_core)
    put_x(x_own, 0, h * per_core, mine)
    put_x(pair, per_core, (1 - h) * per_core)

    row = lax.broadcasted_iota(jnp.int32, (BLK, BLK), 0)
    col = lax.broadcasted_iota(jnp.int32, (BLK, BLK), 1)
    within = row + col >= BLK - 1
    flip = jnp.where(row + col == BLK - 1, 1.0, 0.0).astype(BF16)

    def one_group(g, _):
        count = level[g]
        x_flip = lax.dot_general(
            flip, x_t[g], (((1,), (1,)), ((), ())), preferred_element_type=F32
        ).astype(BF16)
        acc = jnp.zeros((blocks * CPG, BLK), F32)
        held = []

        def diagonals(k):
            now = jnp.where(k < count, held[k], 0.0)
            after = jnp.where(k + 1 < count, held[k + 1], 0.0) if k + 1 < NOFF else 0.0
            skew = pltpu.roll(jnp.where(within, now, after), 1, 1, stride=1, stride_axis=0)
            dh_ref[g, k] = jnp.sum(skew.reshape(BLK // 8, 8, BLK), axis=0)

        for two in range(0, NOFF, 2):
            window = dy_t[g, CPG + two * CPG : CPG + (two + blocks) * CPG, :]
            tile = tile_ref[g, two * BLK : (two + 2) * BLK, :]
            acc = acc + jnp.dot(window, tile, preferred_element_type=F32)
            product = jnp.dot(x_flip, window, preferred_element_type=F32)
            held += [product[:, :BLK], product[:, BLK:]]
            if two:
                diagonals(two - 1)
            diagonals(two)
        diagonals(NOFF - 1)
        dx_ref[:, aligned(g * CPG, CPG), :] = acc.reshape(blocks, CPG, BLK).astype(BF16)
        return 0

    lax.fori_loop(0, groups, one_group, 0)

    sums = jnp.sum(dh_ref[...], axis=2)
    lane = lax.broadcasted_iota(jnp.int32, (NOFF, LANES), 1) // QUART
    for q in range(4):
        for p in range(groups // 4):
            packed = jnp.zeros((NOFF, LANES), F32)
            for m in range(4):
                moved = pltpu.roll(sums[4 * p + m], (m - q) % 4 * QUART, 1)
                packed = jnp.where(lane == m, moved, packed)
            send_ref[:, q * (groups // 4) + p, :] = packed


def filter_kernel(scale, got, out):
    total = jnp.sum(got[...], axis=0) * scale
    for i in range(4):
        for m in range(4):
            out[4 * i + m : 4 * i + m + 1, :] = total[i : i + 1, m * QUART : (m + 1) * QUART]


def widen_kernel(got, out):
    cores = 2
    grps = got.shape[0] // cores
    for h in range(cores):
        for r in range(grps):
            at = (r * cores + h) * LANES
            out[:, at : at + LANES] = got[h * grps + r].T


def call(kernel, name, outs, in_specs, scratch=()):
    return pl.pallas_call(
        kernel,
        out_shape=outs,
        in_specs=in_specs,
        out_specs=jax.tree.map(lambda _: VMEM, outs),
        scratch_shapes=scratch,
        compiler_params=PARAMS,
        name=name,
    )


def per_device(inputs, out_grad, filt, band):
    rows, channels = inputs.shape
    groups = channels // CPG // 2
    blocks = 2 * rows // BLK
    chips = lax.axis_size("chip")
    h = lax.axis_index("core")
    seq = ("chip", "core")

    def lanes(whole, which):
        return lax.dynamic_slice_in_dim(whole, which * LANES, LANES, 1)

    def earlier_chip(block, swap):
        pairs = [(2 * c + o, 2 * (c - 1) + (o ^ swap)) for c in range(1, chips) for o in range(2)]
        return lax.ppermute(block, seq, pairs)

    def other_core(block):
        return lax.ppermute(block, "core", [(0, 1), (1, 0)])

    give = lanes(out_grad, 1 - h)
    later_same = earlier_chip(lanes(out_grad, h), 0)
    later_other = earlier_chip(give, 1)
    pair = other_core(jnp.concatenate([give, lanes(inputs, 1 - h)], axis=0))

    level = lax.dynamic_slice_in_dim(jnp.sum(band, axis=1), h * groups, groups, 0)
    my_filt = lax.dynamic_slice_in_dim(filt, h * groups, groups, 0)
    turned = my_filt.reshape(groups, NOFF, BLK)[:, :, ::-1].astype(F32)
    tile = call(
        tiles_kernel,
        "tiles",
        jax.ShapeDtypeStruct((groups, NOFF * BLK, BLK), BF16),
        [SMEM, VMEM],
    )(level, turned)
    dx, send = call(
        main_kernel,
        "main",
        (
            jax.ShapeDtypeStruct((blocks, LANES, BLK), BF16),
            jax.ShapeDtypeStruct((NOFF, groups, LANES), F32),
        ),
        [SMEM, SMEM] + [VMEM] * 6,
        [
            pltpu.VMEM((groups, (2 * blocks + 1) * CPG, 2 * BLK), BF16),
            pltpu.VMEM((groups, blocks * CPG, BLK), BF16),
            pltpu.VMEM((groups, NOFF, 8, BLK), F32),
        ],
    )(level, h[None], tile, out_grad, inputs, pair, later_same, later_other)

    got = lax.all_to_all(send.reshape(2 * chips, groups // 4, LANES), seq, 0, 0, tiled=True)
    wide = lax.all_to_all(dx, ("core", "grp"), 0, 0, tiled=True)
    scale = 1.0 / math.sqrt(rows * 2 * chips * CPG)
    filter_grad = call(
        functools.partial(filter_kernel, scale),
        "filter",
        jax.ShapeDtypeStruct((2 * groups, QUART), F32),
        [VMEM],
    )(got.reshape(chips, groups // 2, LANES))
    input_grad = call(
        widen_kernel, "widen", jax.ShapeDtypeStruct((BLK, blocks * LANES), BF16), [VMEM]
    )(wide)
    return input_grad, filter_grad


def solution(mesh):
    seq, grp = mesh.shape["seq"], mesh.shape["grp"]
    split = Mesh(mesh.devices.reshape(seq // 2, 2, grp), ("chip", "core", "grp"))
    return jax.shard_map(
        per_device,
        mesh=split,
        in_specs=(
            P(("chip", "core"), "grp"),
            P(("chip", "core"), "grp"),
            P("grp", None),
            P("grp", None),
        ),
        out_specs=(P(("chip", "core", "grp"), None), P("grp", ("chip", "core"))),
        check_vma=False,
    )
```

time: 642 us -> 85.3 us (0.13)
  the two profiles are of different devices: /device:TPU:8 before, /device:TPU:1 now
where the time goes in v1:
time: 85.3 us; the launch traced here: 84.8 us
  blocking collectives  29.6 us (35%)
  waiting for transfers between devices  19.1 us (22%)
  starting transfers between devices  16.3 us (19%)
  Pallas kernels  13.9 us (16%)
  local copies, waits for them, and re-layouts  4.26 us (5%)
  other arithmetic  0.86 us (1%)
    all_to_all x1, blocking collectives, per_device(): lax.all_to_all(send.reshape(2 * chips, groups // 4, LANES), seq, 0, 0, ti...  29.6 us
    pallas_call x1, Pallas kernels, per_device(): call(main_kernel, 'main', (jax.ShapeDtypeStruct((blocks, LANES, BLK), BF1...  10 us
    all_to_all x1, waiting for transfers between devices, per_device(): wide = lax.all_to_all(dx, ('core', 'grp'), 0, 0, tiled=True)  9.85 us
    ppermute x2, waiting for transfers between devices, earlier_chip(): return lax.ppermute(block, seq, pairs)  9.28 us
    ppermute x1, starting transfers between devices, other_core(): return lax.ppermute(block, 'core', [(0, 1), (1, 0)])  8.79 us
    all_to_all x1, starting transfers between devices, per_device(): wide = lax.all_to_all(dx, ('core', 'grp'), 0, 0, tiled=True)  4.92 us
    ppermute x2, starting transfers between devices, earlier_chip(): return lax.ppermute(block, seq, pairs)  2.58 us
    pallas_call x1, Pallas kernels, per_device(): call(tiles_kernel, 'tiles', jax.ShapeDtypeStruct((groups, NOFF * BLK, BLK...  2.21 us
  transfers between devices with their start and end apart: 4, of which 3 were waited for; matrix products, arithmetic and copies ran while one was open for 1% of the time, Pallas kernels for 3%

profile of v1, /device:TPU:1, one launch (start us, length us, event | category | flops | bytes accessed | tf_op | source)
XLA Modules:
  0.0 84.8 jit_solution(9913544237431289113)
XLA Ops:
  0.6 0.0 copy-start
  0.6 0.0 copy-start.3
  0.7 0.0 copy-start.2
  0.7 1.1 %constant_dynamic-slice_fusion.1 = bf16[1024,128]{1,0:T(8,128)(2,1)S(1)} fusion(bf16[1024,256]{1,0:T(8,128)(2,1)} %x_own.1, s32[]{:T(128)S(6)} %select_n.12), kind=kLoop, calls=%fused_computation.4 | loop fusion | bytes 524292 | tf_op jit(solution)/shard_map/dynamic_slice | solution.py:160
  1.7 1.1 %constant_dynamic-slice_fusion = (bf16[1024,128]{1,0:T(8,128)(2,1)S(1)}, bf16[1024,128]{1,0:T(8,128)(2,1)S(1)}) fusion(bf16[1024,256]{1,0:T(8,128)(2,1)} %dy_own.1, s32[]{:T(128)S(6)} %select_n.13, s32[]{:T(128)S(6)} %select_n.12), kind=kLoop, calls=%fused_computation.3 | loop fusion | bytes 1048584 | tf_op jit(solution)/shard_map/dynamic_slice | solution.py:160
  2.9 8.8 %collective-permute-start = (bf16[2048,128]{1,0:T(8,128)(2,1)S(1)}, bf16[2048,128]{1,0:T(8,128)(2,1)S(1)}, u32[]{:S(2)}, u32[]{:S(2)}) collective-permute-start(bf16[2048,128]{1,0:T(8,128)(2,1)S(1)} %pad_maximum_fusion), channel_id=1, source_target_pairs={{0,8},{8,0},{1,9},{9,1},{2,10},{10,2},{3,11},{11,3},{4,12},{12,4},... | collective-permute-start | bytes 1572872 | tf_op jit(solution)/shard_map/ppermute | solution.py:167
  11.7 1.3 %collective-permute-start.1 = (bf16[1024,128]{1,0:T(8,128)(2,1)S(1)}, bf16[1024,128]{1,0:T(8,128)(2,1)S(1)}, u32[]{:S(2)}, u32[]{:S(2)}) collective-permute-start(bf16[1024,128]{1,0:T(8,128)(2,1)S(1)} %get-tuple-element.6), channel_id=1, source_target_pairs={{16,0},{24,8},{32,16},{40,24},{48,32},{56,40},{64,48},{72,56},{80,... | collective-permute-start | bytes 786440 | tf_op jit(solution)/shard_map/ppermute | solution.py:164
  13.0 1.3 %collective-permute-start.2 = (bf16[1024,128]{1,0:T(8,128)(2,1)S(1)}, bf16[1024,128]{1,0:T(8,128)(2,1)S(1)}, u32[]{:S(2)}, u32[]{:S(2)}) collective-permute-start(bf16[1024,128]{1,0:T(8,128)(2,1)S(1)} %get-tuple-element.7), channel_id=1, source_target_pairs={{16,8},{24,0},{32,24},{40,16},{48,40},{56,32},{64,56},{72,48},{80,... | collective-permute-start | bytes 786440 | tf_op jit(solution)/shard_map/ppermute | solution.py:164
  14.3 0.8 reduce_sum.9
  15.1 0.1 dynamic_slice.15.level
  15.1 0.0 copy-done
  15.2 0.1 rev.3
  15.3 2.2 %tiles.1.tile_ref = bf16[8,2048,128]{2,1,0:T(8,128)(2,1)S(1)} custom-call(s32[8]{0:T(128)S(1)} %dynamic_slice.15.level, f32[8,16,128]{2,1,0:T(8,128)S(1)} %convert_element_type.3.turned_filt), custom_call_target="tpu_custom_call" | custom-call | tf_op jit(solution)/shard_map/tiles/pallas_call | solution.py:177
  17.5 0.0 copy-start.1
  17.5 1.9 %copy-done.1 = bf16[8,2048,128]{2,1,0:T(8,128)(2,1)} copy-done((bf16[8,2048,128]{2,1,0:T(8,128)(2,1)}, bf16[8,2048,128]{2,1,0:T(8,128)(2,1)S(1)}, u32[]{:S(2)}) %copy-start.1) | copy-done | bytes 4194328
  19.4 3.6 %collective-permute-done.1.later_same = bf16[1024,128]{1,0:T(8,128)(2,1)S(1)} collective-permute-done((bf16[1024,128]{1,0:T(8,128)(2,1)S(1)}, bf16[1024,128]{1,0:T(8,128)(2,1)S(1)}, u32[]{:S(2)}, u32[]{:S(2)}) %collective-permute-start.1) | collective-permute-done | bytes 262176 | tf_op jit(solution)/shard_map/ppermute | solution.py:164
  23.0 5.7 %collective-permute-done.2.later_other = bf16[1024,128]{1,0:T(8,128)(2,1)S(1)} collective-permute-done((bf16[1024,128]{1,0:T(8,128)(2,1)S(1)}, bf16[1024,128]{1,0:T(8,128)(2,1)S(1)}, u32[]{:S(2)}, u32[]{:S(2)}) %collective-permute-start.2) | collective-permute-done | bytes 262176 | tf_op jit(solution)/shard_map/ppermute | solution.py:164
  28.7 0.0 collective-permute-done.pair
  28.7 10.0 %main.1 = (bf16[16,128,128]{2,1,0:T(8,128)(2,1)}, f32[16,8,128]{2,1,0:T(8,128)S(1)}) custom-call(s32[8]{0:T(128)S(1)} %dynamic_slice.15.level, s32[1]{0:T(128)} %bitcast.core, bf16[8,2048,128]{2,1,0:T(8,128)(2,1)} %copy-done.1, bf16[1024,256]{1,0:T(8,128)(2,1)S(1)} %copy-done.2, bf16[1024,256]{1,0:T(8,128)(2,1)S(1)} %copy-done.3, ...), custom_call_target="tpu_custom_call" | custom-call | tf_op jit(solution)/shard_map/main/pallas_call | solution.py:183
  38.8 29.6 %all_to_all.10 = f32[64,2,128]{2,1,0:T(2,128)S(1)} all-to-all(f32[64,2,128]{2,1,0:T(2,128)S(1)} %bitcast.9), channel_id=1, replica_groups=mesh['chip'=32,'core'=2,'grp'=8] {'chip','core'}, dimensions={0} | all-to-all | bytes 131072 | tf_op jit(solution)/shard_map/all_to_all | solution.py:198
  68.4 4.9 %all-to-all-start = ((bf16[16,128,128]{2,1,0:T(8,128)(2,1)}), bf16[16,128,128]{2,1,0:T(8,128)(2,1)S(1)}, u32[]{:S(2)}, u32[]{:S(2)}) async-start(bf16[16,128,128]{2,1,0:T(8,128)(2,1)} %get-tuple-element.4), calls=%async_computation | async-start | bytes 1048576 | tf_op jit(solution)/shard_map/all_to_all | solution.py:199
  73.3 0.7 filter.1
  74.0 9.9 %all-to-all-done.got = bf16[16,128,128]{2,1,0:T(8,128)(2,1)S(1)} async-done(((bf16[16,128,128]{2,1,0:T(8,128)(2,1)}), bf16[16,128,128]{2,1,0:T(8,128)(2,1)S(1)}, u32[]{:S(2)}, u32[]{:S(2)}) %all-to-all-start) | async-done | bytes 524320 | tf_op jit(solution)/shard_map/all_to_all | solution.py:199
  83.9 1.0 %widen.1 = bf16[128,2048]{1,0:T(8,128)(2,1)} custom-call(bf16[16,128,128]{2,1,0:T(8,128)(2,1)S(1)} %all-to-all-done.got), custom_call_target="tpu_custom_call" | custom-call | tf_op jit(solution)/shard_map/widen/pallas_call | solution.py:207
  (6 shorter events, 0.1 us)
Async XLA Ops:
  0.6 14.5 %copy-start = (bf16[16,2048]{1,0:T(8,128)(2,1)S(1)}, bf16[16,2048]{1,0:T(8,128)(2,1)}, u32[]{:S(2)}) copy-start(bf16[16,2048]{1,0:T(8,128)(2,1)} %param.6) | copy-start | bytes 196612
  0.6 28.1 %copy-start.3 = (bf16[1024,256]{1,0:T(8,128)(2,1)S(1)}, bf16[1024,256]{1,0:T(8,128)(2,1)}, u32[]{:S(2)}) copy-start(bf16[1024,256]{1,0:T(8,128)(2,1)} %x_own.1) | copy-start | bytes 1572868
  0.7 28.1 %copy-start.2 = (bf16[1024,256]{1,0:T(8,128)(2,1)S(1)}, bf16[1024,256]{1,0:T(8,128)(2,1)}, u32[]{:S(2)}) copy-start(bf16[1024,256]{1,0:T(8,128)(2,1)} %dy_own.1) | copy-start | bytes 1572868
  2.9 25.8 %collective-permute-start = (bf16[2048,128]{1,0:T(8,128)(2,1)S(1)}, bf16[2048,128]{1,0:T(8,128)(2,1)S(1)}, u32[]{:S(2)}, u32[]{:S(2)}) collective-permute-start(bf16[2048,128]{1,0:T(8,128)(2,1)S(1)} %pad_maximum_fusion), channel_id=1, source_target_pairs={{0,8},{8,0},{1,9},{9,1},{2,10},{10,2},{3,11},{11,3},{4,12},{12,4},... | collective-permute-start | bytes 1572872 | tf_op jit(solution)/shard_map/ppermute | solution.py:167
  11.7 11.3 %collective-permute-start.1 = (bf16[1024,128]{1,0:T(8,128)(2,1)S(1)}, bf16[1024,128]{1,0:T(8,128)(2,1)S(1)}, u32[]{:S(2)}, u32[]{:S(2)}) collective-permute-start(bf16[1024,128]{1,0:T(8,128)(2,1)S(1)} %get-tuple-element.6), channel_id=1, source_target_pairs={{16,0},{24,8},{32,16},{40,24},{48,32},{56,40},{64,48},{72,56},{80,... | collective-permute-start | bytes 786440 | tf_op jit(solution)/shard_map/ppermute | solution.py:164
  13.0 15.7 %collective-permute-start.2 = (bf16[1024,128]{1,0:T(8,128)(2,1)S(1)}, bf16[1024,128]{1,0:T(8,128)(2,1)S(1)}, u32[]{:S(2)}, u32[]{:S(2)}) collective-permute-start(bf16[1024,128]{1,0:T(8,128)(2,1)S(1)} %get-tuple-element.7), channel_id=1, source_target_pairs={{16,8},{24,0},{32,24},{40,16},{48,40},{56,32},{64,56},{72,48},{80,... | collective-permute-start | bytes 786440 | tf_op jit(solution)/shard_map/ppermute | solution.py:164
  17.5 1.9 %copy-start.1 = (bf16[8,2048,128]{2,1,0:T(8,128)(2,1)}, bf16[8,2048,128]{2,1,0:T(8,128)(2,1)S(1)}, u32[]{:S(2)}) copy-start(bf16[8,2048,128]{2,1,0:T(8,128)(2,1)S(1)} %tiles.1.tile_ref) | copy-start | bytes 12582916
  68.4 15.5 %all-to-all-start = ((bf16[16,128,128]{2,1,0:T(8,128)(2,1)}), bf16[16,128,128]{2,1,0:T(8,128)(2,1)S(1)}, u32[]{:S(2)}, u32[]{:S(2)}) async-start(bf16[16,128,128]{2,1,0:T(8,128)(2,1)} %get-tuple-element.4), calls=%async_computation | async-start | bytes 1048576 | tf_op jit(solution)/shard_map/all_to_all | solution.py:199

commit v2 on v1

v2 whole, which is shorter than its diff:
```python
import functools
import math

import jax
import jax.numpy as jnp
from jax import lax
from jax.experimental import pallas as pl
from jax.experimental.pallas import tpu as pltpu
from jax.sharding import Mesh
from jax.sharding import PartitionSpec as P

CPG = 16
BLK = 128
NOFF = 16
LANES = 128
QUART = 32
BF16 = jnp.bfloat16
F32 = jnp.float32
VMEM = pl.BlockSpec(memory_space=pltpu.VMEM)
SMEM = pl.BlockSpec(memory_space=pltpu.SMEM)
PARAMS = pltpu.CompilerParams(vmem_limit_bytes=24 << 20)


def aligned(start, size):
    return pl.ds(pl.multiple_of(start, size), size)


def tiles_kernel(level, turned_filt, tile_ref):
    row = lax.broadcasted_iota(jnp.int32, (BLK, BLK), 0)
    col = lax.broadcasted_iota(jnp.int32, (BLK, BLK), 1)

    def one_group(g, _):
        lags = turned_filt[g]
        before = jnp.zeros((BLK, BLK), F32)
        for k in range(NOFF):
            spread = jnp.broadcast_to(lags[k : k + 1], (BLK, BLK))
            here = pltpu.roll(spread, 1, 1, stride=1, stride_axis=0)
            tile = jnp.where(col > row, before, here)
            tile = jnp.where(k < level[g], tile, 0.0)
            tile_ref[g, k * BLK : (k + 1) * BLK, :] = tile.astype(BF16)
            before = here
        return 0

    lax.fori_loop(0, turned_filt.shape[0], one_group, 0)


def transposed(block):
    return block.T.reshape(-1, CPG, BLK)


def cut_kernel(core, dy, x, keep, give, pair):
    h = core[0]
    rows = dy.shape[0]
    keep[...] = dy[:, aligned(h * LANES, LANES)]
    theirs = aligned((1 - h) * LANES, LANES)
    give[...] = dy[:, theirs]
    pair[:rows] = dy[:, theirs]
    pair[rows:] = x[:, theirs]


def own_kernel(core, dy_own, x_own, pair, dy_out, x_out):
    per_core = dy_own.shape[0] // BLK
    h = core[0]
    mine = aligned(h * LANES, LANES)
    row = lax.broadcasted_iota(jnp.int32, (BLK, BLK), 0)
    col = lax.broadcasted_iota(jnp.int32, (BLK, BLK), 1)
    flip = jnp.where(row + col == BLK - 1, 1.0, 0.0).astype(BF16)

    def run(x_t):
        for i in range(per_core):
            here = pl.ds(i * BLK, BLK)
            first = aligned((h * per_core + i) * CPG, CPG)
            second = aligned(((1 - h) * per_core + i) * CPG, CPG)
            dy_out[:, first, :] = transposed(dy_own[here, mine])
            dy_out[:, second, :] = transposed(pair[here, :])
            x_t[:, first, :] = transposed(x_own[here, mine])
            x_t[:, second, :] = transposed(pair[pl.ds((per_core + i) * BLK, BLK), :])
        for g in range(x_t.shape[0]):
            x_out[g] = lax.dot_general(
                flip, x_t[g], (((1,), (1,)), ((), ())), preferred_element_type=F32
            ).astype(BF16)

    pl.run_scoped(run, pltpu.VMEM(dy_out.shape, BF16))


def window(own, later, g, k):
    if k == 0:
        return own[g]
    return jnp.concatenate([own[g, k * CPG :, :], later[g, : k * CPG, :]], axis=0)


def two_windows(own, later, g, k):
    return jnp.concatenate([window(own, later, g, k), window(own, later, g, k + 1)], axis=1)


def filt_grad_kernel(level, core, x_flip, own, later_same, later_other, send_ref, later, dh_ref):
    groups = own.shape[0]
    per_core = later_same.shape[0] // BLK
    h = core[0]
    for i in range(per_core):
        here = pl.ds(i * BLK, BLK)
        later[:, aligned((h * per_core + i) * CPG, CPG), :] = transposed(later_same[here, :])
        later[:, aligned(((1 - h) * per_core + i) * CPG, CPG), :] = transposed(later_other[here, :])
    row = lax.broadcasted_iota(jnp.int32, (BLK, BLK), 0)
    col = lax.broadcasted_iota(jnp.int32, (BLK, BLK), 1)
    within = row + col >= BLK - 1

    def one_group(g, _):
        count = level[g]
        x_here = x_flip[g]
        held = []

        def diagonals(k):
            now = jnp.where(k < count, held[k], 0.0)
            after = jnp.where(k + 1 < count, held[k + 1], 0.0) if k + 1 < NOFF else 0.0
            skew = pltpu.roll(jnp.where(within, now, after), 1, 1, stride=1, stride_axis=0)
            dh_ref[g, k] = jnp.sum(skew.reshape(BLK // 8, 8, BLK), axis=0)

        for two in range(0, NOFF, 2):
            product = jnp.dot(
                x_here, two_windows(own, later, g, two), preferred_element_type=F32
            )
            held += [product[:, :BLK], product[:, BLK:]]
            if two:
                diagonals(two - 1)
            diagonals(two)
        diagonals(NOFF - 1)
        return 0

    lax.fori_loop(0, groups, one_group, 0)

    for g in range(groups):
        send_ref[:, g, :] = jnp.sum(dh_ref[g], axis=1)


def in_grad_kernel(tile_ref, own, later, dx_ref):
    groups = own.shape[0]

    def one_group(g, _):
        acc = None
        for two in range(0, NOFF, 2):
            part = jnp.dot(
                two_windows(own, later, g, two),
                tile_ref[g, two * BLK : (two + 2) * BLK, :],
                preferred_element_type=F32,
            )
            acc = part if acc is None else acc + part
        dx_ref[:, aligned(g * CPG, CPG), :] = acc.reshape(-1, CPG, BLK).astype(BF16)
        return 0

    lax.fori_loop(0, groups, one_group, 0)


def join_kernel(scale, place, mine, theirs, out):
    core, shift = place[0], place[1]
    groups = mine.shape[0]
    for at, part in ((core, mine), (1 - core, theirs)):
        out[aligned(at * groups, groups), :] = pltpu.roll(part[...], shift, 1)[:, :QUART] * scale


def widen_kernel(got, out):
    cores = 2
    grps = got.shape[0] // cores
    for h in range(cores):
        for r in range(grps):
            at = (r * cores + h) * LANES
            out[:, at : at + LANES] = got[h * grps + r].T


def call(kernel, name, outs, in_specs, scratch=()):
    return pl.pallas_call(
        kernel,
        out_shape=outs,
        in_specs=in_specs,
        out_specs=jax.tree.map(lambda _: VMEM, outs),
        scratch_shapes=scratch,
        compiler_params=PARAMS,
        name=name,
    )


def per_device(inputs, out_grad, filt, band):
    rows, channels = inputs.shape
    groups = channels // CPG // 2
    blocks = 2 * rows // BLK
    chips = 2 * lax.axis_size("z")
    h = lax.axis_index("core")
    seq = ("z", "xh", "core")

    def earlier_chip(block, swap):
        pairs = [(2 * c + o, 2 * (c - 1) + (o ^ swap)) for c in range(1, chips) for o in range(2)]
        return lax.ppermute(block, seq, pairs)

    half = jax.ShapeDtypeStruct((rows, LANES), BF16)
    keep, give, pair = call(
        cut_kernel,
        "cut",
        (half, half, jax.ShapeDtypeStruct((2 * rows, LANES), BF16)),
        [SMEM, VMEM, VMEM],
    )(h[None], out_grad, inputs)
    later_same = earlier_chip(keep, 0)
    later_other = earlier_chip(give, 1)
    pair = lax.ppermute(pair, "core", [(0, 1), (1, 0)])

    level = lax.dynamic_slice_in_dim(jnp.sum(band, axis=1), h * groups, groups, 0)
    my_filt = lax.dynamic_slice_in_dim(filt, h * groups, groups, 0)
    turned = my_filt.reshape(groups, NOFF, BLK)[:, :, ::-1].astype(F32)
    tile = call(
        tiles_kernel,
        "tiles",
        jax.ShapeDtypeStruct((groups, NOFF * BLK, BLK), BF16),
        [SMEM, VMEM],
    )(level, turned)
    turned_shape = jax.ShapeDtypeStruct((groups, blocks * CPG, BLK), BF16)
    own, x_flip = call(
        own_kernel,
        "own",
        (turned_shape, jax.ShapeDtypeStruct((groups, BLK, blocks * CPG), BF16)),
        [SMEM] + [VMEM] * 3,
    )(h[None], out_grad, inputs, pair)
    send, later = call(
        filt_grad_kernel,
        "filt_grad",
        (jax.ShapeDtypeStruct((NOFF, groups, LANES), F32), turned_shape),
        [SMEM, SMEM] + [VMEM] * 4,
        [pltpu.VMEM((groups, NOFF, 8, BLK), F32)],
    )(level, h[None], x_flip, own, later_same, later_other)
    dx = call(
        in_grad_kernel,
        "in_grad",
        jax.ShapeDtypeStruct((blocks, LANES, BLK), BF16),
        [VMEM] * 3,
    )(tile, own, later)

    got = lax.all_to_all(send, "z", 0, 0, tiled=True)
    wide = lax.all_to_all(dx, ("core", "grp"), 0, 0, tiled=True)
    swap = [(0, 1), (1, 0)]
    total = jnp.sum(got, axis=0)
    total = total + lax.ppermute(total, "xh", swap)
    theirs = lax.ppermute(total, "core", swap)
    shift = (LANES - (2 * lax.axis_index("xh") + h) * QUART) % LANES
    scale = 1.0 / math.sqrt(rows * 2 * chips * CPG)
    filter_grad = call(
        functools.partial(join_kernel, scale),
        "join",
        jax.ShapeDtypeStruct((2 * groups, QUART), F32),
        [SMEM, VMEM, VMEM],
    )(jnp.stack([h, shift]), total, theirs)
    input_grad = call(
        widen_kernel, "widen", jax.ShapeDtypeStruct((BLK, blocks * LANES), BF16), [VMEM]
    )(wide)
    return input_grad, filter_grad


def solution(mesh):
    seq, grp = mesh.shape["seq"], mesh.shape["grp"]
    split = Mesh(mesh.devices.reshape(seq // 4, 2, 2, grp), ("z", "xh", "core", "grp"))
    tokens = ("z", "xh", "core")
    return jax.shard_map(
        per_device,
        mesh=split,
        in_specs=(P(tokens, "grp"), P(tokens, "grp"), P("grp", None), P("grp", None)),
        out_specs=(P(tokens + ("grp",), None), P("grp", tokens)),
        check_vma=False,
    )
```

time: 85.3 us -> 79.4 us (0.931)
  blocking collectives: 29.6 us -> 0 us
  starting transfers between devices: 16.3 us -> 36.2 us
  waiting for transfers between devices: 19.1 us -> 21.7 us
  Pallas kernels: 13.9 us -> 14.9 us
    all_to_all x1 -> x0, blocking collectives: 29.6 us -> none  [per_device(): lax.all_to_all(send.reshape(2 * chips, groups // 4, LANES), seq, 0, 0, ti...]
    all_to_all x1, waiting for transfers between devices: 9.85 us -> 0.01 us  [per_device(): wide = lax.all_to_all(dx, ('core', 'grp'), 0, 0, tiled=True)]
    all_to_all x0 -> x1, starting transfers between devices: none -> 9.54 us  [per_device(): got = lax.all_to_all(send, 'z', 0, 0, tiled=True)]
    ppermute x1 -> x3, starting transfers between devices: 8.79 us -> 16.5 us  [the longest x1 8.79 us: per_device(): pair = lax.ppermute(pair, 'core', [(0, 1), (1, 0)])]
    ppermute x1 -> x3, waiting for transfers between devices: 0.01 us -> 5.72 us  [the longest x1 4.99 us: per_device(): total = total + lax.ppermute(total, 'xh', swap)]
    all_to_all x0 -> x1, waiting for transfers between devices: none -> 5.03 us  [per_device(): got = lax.all_to_all(send, 'z', 0, 0, tiled=True)]
    all_to_all x1, starting transfers between devices: 4.92 us -> 7.5 us  [per_device(): wide = lax.all_to_all(dx, ('core', 'grp'), 0, 0, tiled=True)]
    unnamed x10 -> x12, local copies, waits for them, and re-layouts: 1.96 us -> 4.22 us
  transfers between devices with their start and end apart: 4 -> 7, of which waited for: 3 -> 5; matrix products, arithmetic and copies ran while one was open for 1% -> 1% of each run, Pallas kernels for 3% -> 10%
where the time goes in v2:
time: 79.4 us; the launch traced here: 78.8 us
  starting transfers between devices  36.2 us (46%)
  waiting for transfers between devices  21.7 us (27%)
  Pallas kernels  14.9 us (19%)
  local copies, waits for them, and re-layouts  4.39 us (6%)
  other arithmetic  0.92 us (1%)
    ppermute x2, waiting for transfers between devices, earlier_chip(): return lax.ppermute(block, seq, pairs)  10.9 us
    all_to_all x1, starting transfers between devices, per_device(): got = lax.all_to_all(send, 'z', 0, 0, tiled=True)  9.54 us
    ppermute x1, starting transfers between devices, per_device(): pair = lax.ppermute(pair, 'core', [(0, 1), (1, 0)])  8.79 us
    all_to_all x1, starting transfers between devices, per_device(): wide = lax.all_to_all(dx, ('core', 'grp'), 0, 0, tiled=True)  7.5 us
    pallas_call x1, Pallas kernels, per_device(): call(filt_grad_kernel, 'filt_grad', (jax.ShapeDtypeStruct((NOFF, groups,...  5.58 us
    ppermute x1, starting transfers between devices, per_device(): total = total + lax.ppermute(total, 'xh', swap)  5.28 us
    all_to_all x1, waiting for transfers between devices, per_device(): got = lax.all_to_all(send, 'z', 0, 0, tiled=True)  5.03 us
    ppermute x1, waiting for transfers between devices, per_device(): total = total + lax.ppermute(total, 'xh', swap)  4.99 us
  transfers between devices with their start and end apart: 7, of which 5 were waited for; matrix products, arithmetic and copies ran while one was open for 1% of the time, Pallas kernels for 10%

profile of v2, /device:TPU:1, one launch (start us, length us, event | category | flops | bytes accessed | tf_op | source)
XLA Modules:
  0.0 78.8 jit_solution(17860725884648233737)
XLA Ops:
  0.7 1.1 %copy-done.1 = bf16[1024,256]{1,0:T(8,128)(2,1)S(1)} copy-done((bf16[1024,256]{1,0:T(8,128)(2,1)S(1)}, bf16[1024,256]{1,0:T(8,128)(2,1)}, u32[]{:S(2)}) %copy-start.1) | copy-done | bytes 524312
  1.7 1.0 %copy-done.3 = bf16[1024,256]{1,0:T(8,128)(2,1)S(1)} copy-done((bf16[1024,256]{1,0:T(8,128)(2,1)S(1)}, bf16[1024,256]{1,0:T(8,128)(2,1)}, u32[]{:S(2)}) %copy-start.3) | copy-done | bytes 524312
  2.8 0.2 cut.1
  2.9 8.8 %collective-permute-start = (bf16[2048,128]{1,0:T(8,128)(2,1)S(1)}, bf16[2048,128]{1,0:T(8,128)(2,1)S(1)}, u32[]{:S(2)}, u32[]{:S(2)}) collective-permute-start(bf16[2048,128]{1,0:T(8,128)(2,1)S(1)} %get-tuple-element.9), channel_id=1, source_target_pairs={{0,8},{8,0},{1,9},{9,1},{2,10},{10,2},{3,11},{11,3},{4,12},{12,4},... | collective-permute-start | bytes 1572872 | tf_op jit(solution)/shard_map/ppermute | solution.py:203
  11.7 1.3 %collective-permute-start.1 = (bf16[1024,128]{1,0:T(8,128)(2,1)S(1)}, bf16[1024,128]{1,0:T(8,128)(2,1)S(1)}, u32[]{:S(2)}, u32[]{:S(2)}) collective-permute-start(bf16[1024,128]{1,0:T(8,128)(2,1)S(1)} %get-tuple-element.12), channel_id=1, source_target_pairs={{16,0},{24,8},{32,16},{40,24},{48,32},{56,40},{64,48},{72,56},{80,... | collective-permute-start | bytes 786440 | tf_op jit(solution)/shard_map/ppermute | solution.py:192
  13.0 1.3 %collective-permute-start.2 = (bf16[1024,128]{1,0:T(8,128)(2,1)S(1)}, bf16[1024,128]{1,0:T(8,128)(2,1)S(1)}, u32[]{:S(2)}, u32[]{:S(2)}) collective-permute-start(bf16[1024,128]{1,0:T(8,128)(2,1)S(1)} %get-tuple-element.13), channel_id=1, source_target_pairs={{16,8},{24,0},{32,24},{40,16},{48,40},{56,32},{64,56},{72,48},{80,... | collective-permute-start | bytes 786440 | tf_op jit(solution)/shard_map/ppermute | solution.py:192
  14.3 0.8 %reduce_sum.18 = s32[16]{0:T(128)S(1)} reduce(s32[16,16]{1,0:T(8,128)} %param.7, s32[]{:T(128)} %constant.11.clone.1), dimensions={1}, to_apply=%region_0.0 | reduce | flops 240 | bytes 1092 | tf_op jit(solution)/shard_map/reduce_sum | solution.py:205
  15.2 1.0 %copy-done.2 = bf16[1024,256]{1,0:T(8,128)(2,1)S(1)} copy-done((bf16[1024,256]{1,0:T(8,128)(2,1)S(1)}, bf16[1024,256]{1,0:T(8,128)(2,1)}, u32[]{:S(2)}) %copy-start.2) | copy-done | bytes 524312
  16.3 1.0 %copy-done.4 = bf16[1024,256]{1,0:T(8,128)(2,1)S(1)} copy-done((bf16[1024,256]{1,0:T(8,128)(2,1)S(1)}, bf16[1024,256]{1,0:T(8,128)(2,1)}, u32[]{:S(2)}) %copy-start.4) | copy-done | bytes 524312
  17.3 0.5 own.1
  17.8 5.2 %collective-permute-done.1.later_same = bf16[1024,128]{1,0:T(8,128)(2,1)S(1)} collective-permute-done((bf16[1024,128]{1,0:T(8,128)(2,1)S(1)}, bf16[1024,128]{1,0:T(8,128)(2,1)S(1)}, u32[]{:S(2)}, u32[]{:S(2)}) %collective-permute-start.1) | collective-permute-done | bytes 262176 | tf_op jit(solution)/shard_map/ppermute | solution.py:192
  23.0 5.7 %collective-permute-done.2.later_other = bf16[1024,128]{1,0:T(8,128)(2,1)S(1)} collective-permute-done((bf16[1024,128]{1,0:T(8,128)(2,1)S(1)}, bf16[1024,128]{1,0:T(8,128)(2,1)S(1)}, u32[]{:S(2)}, u32[]{:S(2)}) %collective-permute-start.2) | collective-permute-done | bytes 262176 | tf_op jit(solution)/shard_map/ppermute | solution.py:192
  28.8 5.6 %filt_grad.1 = (f32[16,8,128]{2,1,0:T(8,128)}, bf16[8,256,128]{2,1,0:T(8,128)(2,1)S(1)}) custom-call(s32[8]{0:T(128)S(1)} %dynamic_slice.6.level, s32[1]{0:T(128)} %bitcast.core, bf16[8,128,256]{2,1,0:T(8,128)(2,1)S(1)} %get-tuple-element.11.x_flip, bf16[8,256,128]{2,1,0:T(8,128)(2,1)S(1)} %get-tuple-element.10.own, ...), custom_call_target="tpu_custom_call" | custom-call | tf_op jit(solution)/shard_map/filt_grad/pallas_call | solution.py:221
  34.4 9.5 %all-to-all-start.1 = ((f32[16,8,128]{2,1,0:T(8,128)}), f32[16,8,128]{2,1,0:T(8,128)S(1)}, u32[]{:S(2)}, u32[]{:S(2)}) async-start(f32[16,8,128]{2,1,0:T(8,128)} %get-tuple-element.15), calls=%async_computation.1 | async-start | bytes 131072 | tf_op jit(solution)/shard_map/all_to_all | solution.py:235
  44.1 2.2 %tiles.1.tile_ref = bf16[8,2048,128]{2,1,0:T(8,128)(2,1)S(1)} custom-call(s32[8]{0:T(128)S(1)} %dynamic_slice.6.level, f32[8,16,128]{2,1,0:T(8,128)S(1)} %convert_element_type.3.turned_filt), custom_call_target="tpu_custom_call" | custom-call | tf_op jit(solution)/shard_map/tiles/pallas_call | solution.py:208
  46.3 4.2 %in_grad.1 = bf16[16,128,128]{2,1,0:T(8,128)(2,1)} custom-call(bf16[8,2048,128]{2,1,0:T(8,128)(2,1)S(1)} %tiles.1.tile_ref, bf16[8,256,128]{2,1,0:T(8,128)(2,1)S(1)} %get-tuple-element.10.own, bf16[8,256,128]{2,1,0:T(8,128)(2,1)S(1)} %get-tuple-element.14.later), custom_call_target="tpu_custom_call" | custom-call | tf_op jit(solution)/shard_map/in_grad/pallas_call | solution.py:228
  50.5 5.0 %all-to-all-done.1 = f32[16,8,128]{2,1,0:T(8,128)S(1)} async-done(((f32[16,8,128]{2,1,0:T(8,128)}), f32[16,8,128]{2,1,0:T(8,128)S(1)}, u32[]{:S(2)}, u32[]{:S(2)}) %all-to-all-start.1) | async-done | bytes 65568 | tf_op jit(solution)/shard_map/all_to_all | solution.py:235
  55.5 7.5 %all-to-all-start = ((bf16[16,128,128]{2,1,0:T(8,128)(2,1)}), bf16[16,128,128]{2,1,0:T(8,128)(2,1)S(1)}, u32[]{:S(2)}, u32[]{:S(2)}) async-start(bf16[16,128,128]{2,1,0:T(8,128)(2,1)} %in_grad.1), calls=%async_computation | async-start | bytes 1048576 | tf_op jit(solution)/shard_map/all_to_all | solution.py:236
  63.0 5.3 %collective-permute-start.3 = (f32[8,128]{1,0:T(8,128)S(1)}, f32[8,128]{1,0:T(8,128)S(1)}, u32[]{:S(2)}, u32[]{:S(2)}) collective-permute-start(f32[8,128]{1,0:T(8,128)S(1)} %reduce_sum.19), channel_id=1, source_target_pairs={{0,16},{16,0},{1,17},{17,1},{2,18},{18,2},{3,19},{19,3},{4,20},{20... | collective-permute-start | bytes 12296 | tf_op jit(solution)/shard_map/ppermute | solution.py:239
  68.3 5.0 %collective-permute-done.3 = f32[8,128]{1,0:T(8,128)S(1)} collective-permute-done((f32[8,128]{1,0:T(8,128)S(1)}, f32[8,128]{1,0:T(8,128)S(1)}, u32[]{:S(2)}, u32[]{:S(2)}) %collective-permute-start.3) | collective-permute-done | bytes 4128 | tf_op jit(solution)/shard_map/ppermute | solution.py:239
  73.3 2.5 %collective-permute-start.4 = (f32[8,128]{1,0:T(8,128)S(1)}, f32[8,128]{1,0:T(8,128)S(1)}, u32[]{:S(2)}, u32[]{:S(2)}) collective-permute-start(f32[8,128]{1,0:T(8,128)S(1)} %add.17.mine), channel_id=1, source_target_pairs={{0,8},{8,0},{1,9},{9,1},{2,10},{10,2},{3,11},{11,3},{4,12},{12,4},... | collective-permute-start | bytes 12296 | tf_op jit(solution)/shard_map/ppermute | solution.py:240
  75.9 0.7 collective-permute-done.4.theirs
  76.6 1.2 %join.1 = f32[16,32]{1,0:T(8,128)} custom-call(s32[2]{0:T(128)S(1)} %pad_add_fusion.place, f32[8,128]{1,0:T(8,128)S(1)} %add.17.mine, f32[8,128]{1,0:T(8,128)S(1)} %collective-permute-done.4.theirs), custom_call_target="tpu_custom_call" | custom-call | tf_op jit(solution)/shard_map/join/pallas_call | solution.py:243
  77.8 1.0 %widen.1 = bf16[128,2048]{1,0:T(8,128)(2,1)} custom-call(bf16[16,128,128]{2,1,0:T(8,128)(2,1)S(1)} %all-to-all-done.got), custom_call_target="tpu_custom_call" | custom-call | tf_op jit(solution)/shard_map/widen/pallas_call | solution.py:249
  (16 shorter events, 0.3 us)
Async XLA Ops:
  0.6 43.3 %copy-start = (bf16[16,2048]{1,0:T(8,128)(2,1)S(1)}, bf16[16,2048]{1,0:T(8,128)(2,1)}, u32[]{:S(2)}) copy-start(bf16[16,2048]{1,0:T(8,128)(2,1)} %param.6) | copy-start | bytes 196612
  0.7 1.1 %copy-start.1 = (bf16[1024,256]{1,0:T(8,128)(2,1)S(1)}, bf16[1024,256]{1,0:T(8,128)(2,1)}, u32[]{:S(2)}) copy-start(bf16[1024,256]{1,0:T(8,128)(2,1)} %dy_own.1) | copy-start | bytes 1572868
  1.7 1.0 %copy-start.3 = (bf16[1024,256]{1,0:T(8,128)(2,1)S(1)}, bf16[1024,256]{1,0:T(8,128)(2,1)}, u32[]{:S(2)}) copy-start(bf16[1024,256]{1,0:T(8,128)(2,1)} %x_own.1) | copy-start | bytes 1572868
  2.9 12.3 %collective-permute-start = (bf16[2048,128]{1,0:T(8,128)(2,1)S(1)}, bf16[2048,128]{1,0:T(8,128)(2,1)S(1)}, u32[]{:S(2)}, u32[]{:S(2)}) collective-permute-start(bf16[2048,128]{1,0:T(8,128)(2,1)S(1)} %get-tuple-element.9), channel_id=1, source_target_pairs={{0,8},{8,0},{1,9},{9,1},{2,10},{10,2},{3,11},{11,3},{4,12},{12,4},... | collective-permute-start | bytes 1572872 | tf_op jit(solution)/shard_map/ppermute | solution.py:203
  11.7 11.3 %collective-permute-start.1 = (bf16[1024,128]{1,0:T(8,128)(2,1)S(1)}, bf16[1024,128]{1,0:T(8,128)(2,1)S(1)}, u32[]{:S(2)}, u32[]{:S(2)}) collective-permute-start(bf16[1024,128]{1,0:T(8,128)(2,1)S(1)} %get-tuple-element.12), channel_id=1, source_target_pairs={{16,0},{24,8},{32,16},{40,24},{48,32},{56,40},{64,48},{72,56},{80,... | collective-permute-start | bytes 786440 | tf_op jit(solution)/shard_map/ppermute | solution.py:192
  13.0 15.7 %collective-permute-start.2 = (bf16[1024,128]{1,0:T(8,128)(2,1)S(1)}, bf16[1024,128]{1,0:T(8,128)(2,1)S(1)}, u32[]{:S(2)}, u32[]{:S(2)}) collective-permute-start(bf16[1024,128]{1,0:T(8,128)(2,1)S(1)} %get-tuple-element.13), channel_id=1, source_target_pairs={{16,8},{24,0},{32,24},{40,16},{48,40},{56,32},{64,56},{72,48},{80,... | collective-permute-start | bytes 786440 | tf_op jit(solution)/shard_map/ppermute | solution.py:192
  15.2 1.0 %copy-start.2 = (bf16[1024,256]{1,0:T(8,128)(2,1)S(1)}, bf16[1024,256]{1,0:T(8,128)(2,1)}, u32[]{:S(2)}) copy-start(bf16[1024,256]{1,0:T(8,128)(2,1)} %dy_own.1) | copy-start | bytes 1572868
  16.3 1.0 %copy-start.4 = (bf16[1024,256]{1,0:T(8,128)(2,1)S(1)}, bf16[1024,256]{1,0:T(8,128)(2,1)}, u32[]{:S(2)}) copy-start(bf16[1024,256]{1,0:T(8,128)(2,1)} %x_own.1) | copy-start | bytes 1572868
  34.4 21.1 %all-to-all-start.1 = ((f32[16,8,128]{2,1,0:T(8,128)}), f32[16,8,128]{2,1,0:T(8,128)S(1)}, u32[]{:S(2)}, u32[]{:S(2)}) async-start(f32[16,8,128]{2,1,0:T(8,128)} %get-tuple-element.15), calls=%async_computation.1 | async-start | bytes 131072 | tf_op jit(solution)/shard_map/all_to_all | solution.py:235
  55.5 22.3 %all-to-all-start = ((bf16[16,128,128]{2,1,0:T(8,128)(2,1)}), bf16[16,128,128]{2,1,0:T(8,128)(2,1)S(1)}, u32[]{:S(2)}, u32[]{:S(2)}) async-start(bf16[16,128,128]{2,1,0:T(8,128)(2,1)} %in_grad.1), calls=%async_computation | async-start | bytes 1048576 | tf_op jit(solution)/shard_map/all_to_all | solution.py:236
  63.0 10.3 %collective-permute-start.3 = (f32[8,128]{1,0:T(8,128)S(1)}, f32[8,128]{1,0:T(8,128)S(1)}, u32[]{:S(2)}, u32[]{:S(2)}) collective-permute-start(f32[8,128]{1,0:T(8,128)S(1)} %reduce_sum.19), channel_id=1, source_target_pairs={{0,16},{16,0},{1,17},{17,1},{2,18},{18,2},{3,19},{19,3},{4,20},{20... | collective-permute-start | bytes 12296 | tf_op jit(solution)/shard_map/ppermute | solution.py:239
  73.3 3.3 %collective-permute-start.4 = (f32[8,128]{1,0:T(8,128)S(1)}, f32[8,128]{1,0:T(8,128)S(1)}, u32[]{:S(2)}, u32[]{:S(2)}) collective-permute-start(f32[8,128]{1,0:T(8,128)S(1)} %add.17.mine), channel_id=1, source_target_pairs={{0,8},{8,0},{1,9},{9,1},{2,10},{10,2},{3,11},{11,3},{4,12},{12,4},... | collective-permute-start | bytes 12296 | tf_op jit(solution)/shard_map/ppermute | solution.py:240

commit v3 on v2

v3 whole, which is shorter than its diff:
```python
import functools
import math

import jax
import jax.numpy as jnp
from jax import lax
from jax.experimental import pallas as pl
from jax.experimental.pallas import tpu as pltpu
from jax.sharding import Mesh
from jax.sharding import PartitionSpec as P

CPG = 16
BLK = 128
NOFF = 16
LANES = 128
QUART = 32
BF16 = jnp.bfloat16
F32 = jnp.float32
VMEM = pl.BlockSpec(memory_space=pltpu.VMEM)
HBM = pl.BlockSpec(memory_space=pltpu.HBM)
SMEM = pl.BlockSpec(memory_space=pltpu.SMEM)
PARAMS = pltpu.CompilerParams(vmem_limit_bytes=24 << 20)


def aligned(start, size):
    return pl.ds(pl.multiple_of(start, size), size)


def transposed(block):
    return block.T.reshape(-1, CPG, BLK)


def run_copies(sems, *pairs):
    copies = [pltpu.make_async_copy(src, dst, sems.at[i]) for i, (src, dst) in enumerate(pairs)]
    for copy in copies:
        copy.start()
    for copy in copies:
        copy.wait()


def cut_kernel(core, dy, mine, theirs, sems):
    h = core[0]
    run_copies(
        sems,
        (dy.at[:, aligned(h * LANES, LANES)], mine),
        (dy.at[:, aligned((1 - h) * LANES, LANES)], theirs),
    )


def pack_kernel(core, x, dy_theirs, mine, pair, sems):
    h = core[0]
    rows = x.shape[0]
    run_copies(
        sems,
        (x.at[:, aligned(h * LANES, LANES)], mine),
        (dy_theirs, pair.at[:rows]),
        (x.at[:, aligned((1 - h) * LANES, LANES)], pair.at[rows:]),
    )


def own_kernel(core, dy_own, x_own, pair, dy_out, x_out):
    per_core = dy_own.shape[0] // BLK
    h = core[0]
    row = lax.broadcasted_iota(jnp.int32, (BLK, BLK), 0)
    col = lax.broadcasted_iota(jnp.int32, (BLK, BLK), 1)
    flip = jnp.where(row + col == BLK - 1, 1.0, 0.0).astype(BF16)

    def run(x_t):
        for i in range(per_core):
            here = pl.ds(i * BLK, BLK)
            first = aligned((h * per_core + i) * CPG, CPG)
            second = aligned(((1 - h) * per_core + i) * CPG, CPG)
            dy_out[:, first, :] = transposed(dy_own[here, :])
            dy_out[:, second, :] = transposed(pair[here, :])
            x_t[:, first, :] = transposed(x_own[here, :])
            x_t[:, second, :] = transposed(pair[pl.ds((per_core + i) * BLK, BLK), :])
        for g in range(x_t.shape[0]):
            x_out[g] = lax.dot_general(
                flip, x_t[g], (((1,), (1,)), ((), ())), preferred_element_type=F32
            ).astype(BF16)

    pl.run_scoped(run, pltpu.VMEM(dy_out.shape, BF16))


def window(own, later, g, k):
    if k == 0:
        return own[g]
    return jnp.concatenate([own[g, k * CPG :, :], later[g, : k * CPG, :]], axis=0)


def two_windows(own, later, g, k):
    return jnp.concatenate([window(own, later, g, k), window(own, later, g, k + 1)], axis=1)


def filt_grad_kernel(level, core, x_flip, own, later_same, later_other, send_ref, later, dh_ref):
    groups = own.shape[0]
    per_core = later_same.shape[0] // BLK
    h = core[0]
    for i in range(per_core):
        here = pl.ds(i * BLK, BLK)
        later[:, aligned((h * per_core + i) * CPG, CPG), :] = transposed(later_same[here, :])
        later[:, aligned(((1 - h) * per_core + i) * CPG, CPG), :] = transposed(later_other[here, :])
    row = lax.broadcasted_iota(jnp.int32, (BLK, BLK), 0)
    col = lax.broadcasted_iota(jnp.int32, (BLK, BLK), 1)
    within = row + col >= BLK - 1

    for g in range(groups):
        count = level[g]

        def diagonals(k, now, after):
            after = 0.0 if after is None else jnp.where(k + 1 < count, after, 0.0)
            skew = pltpu.roll(jnp.where(within, now, after), 1, 1, stride=1, stride_axis=0)
            eight = jnp.sum(skew.reshape(BLK // 8, 8, BLK), axis=0)
            dh_ref[k, g] = jnp.where(k < count, eight, 0.0)

        last = None
        for two in range(0, NOFF, 2):
            product = jnp.dot(
                x_flip[g], two_windows(own, later, g, two), preferred_element_type=F32
            )
            now, after = product[:, :BLK], product[:, BLK:]
            if two:
                diagonals(two - 1, last, now)
            diagonals(two, now, after)
            last = after
        diagonals(NOFF - 1, last, None)

    sub = lax.broadcasted_iota(jnp.int32, (8, BLK), 0)
    for k in range(NOFF):
        send_ref[k] = column_sums([dh_ref[k, g] for g in range(groups)], sub)


def column_sums(parts, sub):
    for step in (4, 2, 1):
        low = sub % (2 * step) < step
        half = len(parts) // 2
        parts = [
            jnp.where(low, a, b) + pltpu.roll(jnp.where(low, b, a), step, 0)
            if step == 4
            else jnp.where(low, a + pltpu.roll(a, 8 - step, 0), b + pltpu.roll(b, step, 0))
            for a, b in zip(parts[:half], parts[half:])
        ]
    return parts[0]


def in_grad_kernel(level, turned_filt, own, later, dx_ref):
    row = lax.broadcasted_iota(jnp.int32, (BLK, BLK), 0)
    col = lax.broadcasted_iota(jnp.int32, (BLK, BLK), 1)

    def one_group(g, _):
        lags = turned_filt[g]
        before = jnp.zeros((BLK, BLK), F32)
        tiles = []
        for k in range(NOFF):
            spread = jnp.broadcast_to(lags[k : k + 1], (BLK, BLK))
            here = pltpu.roll(spread, 1, 1, stride=1, stride_axis=0)
            tile = jnp.where(col > row, before, here)
            tiles.append(jnp.where(k < level[g], tile, 0.0).astype(BF16))
            before = here
        wide = jnp.concatenate([window(own, later, g, k) for k in range(NOFF)], axis=1)
        grad = jnp.dot(wide, jnp.concatenate(tiles, axis=0), preferred_element_type=F32)
        dx_ref[:, aligned(g * CPG, CPG), :] = grad.reshape(-1, CPG, BLK).astype(BF16)
        return 0

    lax.fori_loop(0, own.shape[0], one_group, 0, unroll=8)


def last_kernel(scale, place, got, mine, theirs, wide, narrow):
    cores = 2
    grps = got.shape[0] // cores
    for h in range(cores):
        for r in range(grps):
            at = (r * cores + h) * LANES
            wide[:, at : at + LANES] = got[h * grps + r].T
    core, shift = place[0], place[1]
    groups = mine.shape[0]
    for at, part in ((core, mine), (1 - core, theirs)):
        narrow[aligned(at * groups, groups), :] = pltpu.roll(part[...], shift, 1)[:, :QUART] * scale


def call(kernel, name, outs, in_specs, scratch=()):
    return pl.pallas_call(
        kernel,
        out_shape=outs,
        in_specs=in_specs,
        out_specs=jax.tree.map(lambda _: VMEM, outs),
        scratch_shapes=scratch,
        compiler_params=PARAMS,
        name=name,
    )


def per_device(inputs, out_grad, filt, band):
    rows, channels = inputs.shape
    groups = channels // CPG // 2
    blocks = 2 * rows // BLK
    chips = 2 * lax.axis_size("z")
    h = lax.axis_index("core")
    seq = ("z", "xh", "core")

    def earlier_chip(block, swap):
        pairs = [(2 * c + o, 2 * (c - 1) + (o ^ swap)) for c in range(1, chips) for o in range(2)]
        return lax.ppermute(block, seq, pairs)

    half = jax.ShapeDtypeStruct((rows, LANES), BF16)

    dy_mine, dy_theirs = call(
        cut_kernel, "cut", (half, half), [SMEM, HBM], [pltpu.SemaphoreType.DMA((2,))]
    )(h[None], out_grad)
    later_same = earlier_chip(dy_mine, 0)
    later_other = earlier_chip(dy_theirs, 1)
    x_mine, pair = call(
        pack_kernel,
        "pack",
        (half, jax.ShapeDtypeStruct((2 * rows, LANES), BF16)),
        [SMEM, HBM, VMEM],
        [pltpu.SemaphoreType.DMA((3,))],
    )(h[None], inputs, dy_theirs)
    swap = [(0, 1), (1, 0)]
    pair = lax.ppermute(pair, "core", swap)
    level = lax.dynamic_slice_in_dim(jnp.sum(band, axis=1), h * groups, groups, 0)
    my_filt = lax.dynamic_slice_in_dim(filt, h * groups, groups, 0)
    turned = my_filt.reshape(groups, NOFF, BLK)[:, :, ::-1].astype(F32)
    turned_shape = jax.ShapeDtypeStruct((groups, blocks * CPG, BLK), BF16)
    own, x_flip = call(
        own_kernel,
        "own",
        (turned_shape, jax.ShapeDtypeStruct((groups, BLK, blocks * CPG), BF16)),
        [SMEM] + [VMEM] * 3,
    )(h[None], dy_mine, x_mine, pair)
    send, later = call(
        filt_grad_kernel,
        "filt_grad",
        (jax.ShapeDtypeStruct((NOFF, groups, LANES), F32), turned_shape),
        [SMEM, SMEM] + [VMEM] * 4,
        [pltpu.VMEM((NOFF, groups, 8, BLK), F32)],
    )(level, h[None], x_flip, own, later_same, later_other)
    dx = call(
        in_grad_kernel,
        "in_grad",
        jax.ShapeDtypeStruct((blocks, LANES, BLK), BF16),
        [SMEM] + [VMEM] * 3,
    )(level, turned, own, later)

    got = lax.all_to_all(send, "z", 0, 0, tiled=True)
    wide = lax.all_to_all(dx, ("core", "grp"), 0, 0, tiled=True)
    total = jnp.sum(got, axis=0)
    total = total + lax.ppermute(total, "xh", swap)
    theirs = lax.ppermute(total, "core", swap)
    shift = (LANES - (2 * lax.axis_index("xh") + h) * QUART) % LANES
    scale = 1.0 / math.sqrt(rows * 2 * chips * CPG)
    return call(
        functools.partial(last_kernel, scale),
        "last",
        (
            jax.ShapeDtypeStruct((BLK, blocks * LANES), BF16),
            jax.ShapeDtypeStruct((2 * groups, QUART), F32),
        ),
        [SMEM] + [VMEM] * 3,
    )(jnp.stack([h, shift]), wide, total, theirs)


def solution(mesh):
    seq, grp = mesh.shape["seq"], mesh.shape["grp"]
    split = Mesh(mesh.devices.reshape(seq // 4, 2, 2, grp), ("z", "xh", "core", "grp"))
    tokens = ("z", "xh", "core")
    return jax.shard_map(
        per_device,
        mesh=split,
        in_specs=(P(tokens, "grp"), P(tokens, "grp"), P("grp", None), P("grp", None)),
        out_specs=(P(tokens + ("grp",), None), P("grp", tokens)),
        check_vma=False,
    )
```

time: 79.4 us -> 77 us (0.970)
  waiting for transfers between devices: 21.7 us -> 27.1 us
  Pallas kernels: 14.9 us -> 10.1 us
  local copies, waits for them, and re-layouts: 4.39 us -> 2.19 us
    ppermute x2, waiting for transfers between devices: 10.9 us -> 13.7 us  [earlier_chip(): return lax.ppermute(block, seq, pairs)]
    pallas_call x4 -> x3, Pallas kernels: 4.56 us -> 1.79 us  [the longest x1 1.54 us: per_device(): call(functools.partial(last_kernel, scale), 'last', (jax.ShapeDtypeStruct...]
    all_to_all x1, waiting for transfers between devices: 5.03 us -> 7.61 us  [per_device(): got = lax.all_to_all(send, 'z', 0, 0, tiled=True)]
    unnamed x12 -> x10, local copies, waits for them, and re-layouts: 4.22 us -> 2.02 us
    pallas_call x1, Pallas kernels: 5.58 us -> 3.97 us  [per_device(): call(filt_grad_kernel, 'filt_grad', (jax.ShapeDtypeStruct((NOFF, groups,...]
  transfers between devices with their start and end apart: 7 -> 7, of which waited for: 5 -> 5; matrix products, arithmetic and copies ran while one was open for 1% -> 1% of each run, Pallas kernels for 10% -> 6%
where the time goes in v3:
time: 77 us; the launch traced here: 76.5 us
  starting transfers between devices  36.2 us (47%)
  waiting for transfers between devices  27.1 us (35%)
  Pallas kernels  10.1 us (13%)
  local copies, waits for them, and re-layouts  2.19 us (3%)
  between operations  0.8 us (1%)
    ppermute x2, waiting for transfers between devices, earlier_chip(): return lax.ppermute(block, seq, pairs)  13.7 us
    all_to_all x1, starting transfers between devices, per_device(): got = lax.all_to_all(send, 'z', 0, 0, tiled=True)  9.54 us
    ppermute x1, starting transfers between devices, per_device(): pair = lax.ppermute(pair, 'core', swap)  8.79 us
    all_to_all x1, waiting for transfers between devices, per_device(): got = lax.all_to_all(send, 'z', 0, 0, tiled=True)  7.61 us
    all_to_all x1, starting transfers between devices, per_device(): wide = lax.all_to_all(dx, ('core', 'grp'), 0, 0, tiled=True)  7.5 us
    ppermute x1, starting transfers between devices, per_device(): total = total + lax.ppermute(total, 'xh', swap)  5.27 us
    ppermute x1, waiting for transfers between devices, per_device(): total = total + lax.ppermute(total, 'xh', swap)  4.99 us
    pallas_call x1, Pallas kernels, per_device(): call(filt_grad_kernel, 'filt_grad', (jax.ShapeDtypeStruct((NOFF, groups,...  3.97 us
  transfers between devices with their start and end apart: 7, of which 5 were waited for; matrix products, arithmetic and copies ran while one was open for 1% of the time, Pallas kernels for 6%

profile of v3, /device:TPU:1, one launch (start us, length us, event | category | flops | bytes accessed | tf_op | source)
XLA Modules:
  0.0 76.5 jit_solution(7741500104763088617)
XLA Ops:
  0.7 1.1 %copy-done.1 = bf16[1024,256]{1,0:T(8,128)(2,1)S(1)} copy-done((bf16[1024,256]{1,0:T(8,128)(2,1)S(1)}, bf16[1024,256]{1,0:T(8,128)(2,1)}, u32[]{:S(2)}) %copy-start.1) | copy-done | bytes 524312
  1.7 0.1 cut.1
  1.8 0.9 %copy-done.2 = bf16[1024,256]{1,0:T(8,128)(2,1)S(1)} copy-done((bf16[1024,256]{1,0:T(8,128)(2,1)S(1)}, bf16[1024,256]{1,0:T(8,128)(2,1)}, u32[]{:S(2)}) %copy-start.2) | copy-done | bytes 524312
  2.8 0.1 pack.1
  2.9 8.8 %collective-permute-start = (bf16[2048,128]{1,0:T(8,128)(2,1)S(1)}, bf16[2048,128]{1,0:T(8,128)(2,1)S(1)}, u32[]{:S(2)}, u32[]{:S(2)}) collective-permute-start(bf16[2048,128]{1,0:T(8,128)(2,1)S(1)} %get-tuple-element.13), channel_id=1, source_target_pairs={{0,8},{8,0},{1,9},{9,1},{2,10},{10,2},{3,11},{11,3},{4,12},{12,4},... | collective-permute-start | bytes 1572872 | tf_op jit(solution)/shard_map/ppermute | solution.py:220
  11.7 1.3 %collective-permute-start.1 = (bf16[1024,128]{1,0:T(8,128)(2,1)S(1)}, bf16[1024,128]{1,0:T(8,128)(2,1)S(1)}, u32[]{:S(2)}, u32[]{:S(2)}) collective-permute-start(bf16[1024,128]{1,0:T(8,128)(2,1)S(1)} %get-tuple-element.10.dy_own), channel_id=1, source_target_pairs={{16,0},{24,8},{32,16},{40,24},{48,32},{56,40},{64,48},{72,56},{80,... | collective-permute-start | bytes 786440 | tf_op jit(solution)/shard_map/ppermute | solution.py:203
  13.0 1.3 %collective-permute-start.2 = (bf16[1024,128]{1,0:T(8,128)(2,1)S(1)}, bf16[1024,128]{1,0:T(8,128)(2,1)S(1)}, u32[]{:S(2)}, u32[]{:S(2)}) collective-permute-start(bf16[1024,128]{1,0:T(8,128)(2,1)S(1)} %get-tuple-element.11.dy_theirs), channel_id=1, source_target_pairs={{16,8},{24,0},{32,24},{40,16},{48,40},{56,32},{64,56},{72,48},{80,... | collective-permute-start | bytes 786440 | tf_op jit(solution)/shard_map/ppermute | solution.py:203
  14.3 0.1 reduce_sum.18
  14.4 0.1 dynamic_slice.6.level
  14.5 0.5 own.1
  15.0 8.0 %collective-permute-done.1.later_same = bf16[1024,128]{1,0:T(8,128)(2,1)S(1)} collective-permute-done((bf16[1024,128]{1,0:T(8,128)(2,1)S(1)}, bf16[1024,128]{1,0:T(8,128)(2,1)S(1)}, u32[]{:S(2)}, u32[]{:S(2)}) %collective-permute-start.1) | collective-permute-done | bytes 262176 | tf_op jit(solution)/shard_map/ppermute | solution.py:203
  23.0 5.7 %collective-permute-done.2.later_other = bf16[1024,128]{1,0:T(8,128)(2,1)S(1)} collective-permute-done((bf16[1024,128]{1,0:T(8,128)(2,1)S(1)}, bf16[1024,128]{1,0:T(8,128)(2,1)S(1)}, u32[]{:S(2)}, u32[]{:S(2)}) %collective-permute-start.2) | collective-permute-done | bytes 262176 | tf_op jit(solution)/shard_map/ppermute | solution.py:203
  28.8 4.0 %filt_grad.1 = (f32[16,8,128]{2,1,0:T(8,128)}, bf16[8,256,128]{2,1,0:T(8,128)(2,1)S(1)}) custom-call(s32[8]{0:T(128)S(1)} %dynamic_slice.6.level, s32[1]{0:T(128)} %bitcast.core, bf16[8,128,256]{2,1,0:T(8,128)(2,1)S(1)} %get-tuple-element.15.x_flip, bf16[8,256,128]{2,1,0:T(8,128)(2,1)S(1)} %get-tuple-element.14.own, ...), custom_call_target="tpu_custom_call" | custom-call | tf_op jit(solution)/shard_map/filt_grad/pallas_call | solution.py:231
  32.7 9.5 %all-to-all-start.1 = ((f32[16,8,128]{2,1,0:T(8,128)}), f32[16,8,128]{2,1,0:T(8,128)S(1)}, u32[]{:S(2)}, u32[]{:S(2)}) async-start(f32[16,8,128]{2,1,0:T(8,128)} %get-tuple-element.17), calls=%async_computation.1 | async-start | bytes 131072 | tf_op jit(solution)/shard_map/all_to_all | solution.py:245
  42.3 0.1 rev.3
  42.4 3.8 %in_grad.1 = bf16[16,128,128]{2,1,0:T(8,128)(2,1)} custom-call(s32[8]{0:T(128)S(1)} %dynamic_slice.6.level, f32[8,16,128]{2,1,0:T(8,128)S(1)} %convert_element_type.3.turned_filt, bf16[8,256,128]{2,1,0:T(8,128)(2,1)S(1)} %get-tuple-element.14.own, bf16[8,256,128]{2,1,0:T(8,128)(2,1)S(1)} %get-tuple-element.16.later), custom_call_target="tpu_custom_call" | custom-call | tf_op jit(solution)/shard_map/in_grad/pallas_call | solution.py:238
  46.3 7.6 %all-to-all-done.1 = f32[16,8,128]{2,1,0:T(8,128)S(1)} async-done(((f32[16,8,128]{2,1,0:T(8,128)}), f32[16,8,128]{2,1,0:T(8,128)S(1)}, u32[]{:S(2)}, u32[]{:S(2)}) %all-to-all-start.1) | async-done | bytes 65568 | tf_op jit(solution)/shard_map/all_to_all | solution.py:245
  53.9 7.5 %all-to-all-start = ((bf16[16,128,128]{2,1,0:T(8,128)(2,1)}), bf16[16,128,128]{2,1,0:T(8,128)(2,1)S(1)}, u32[]{:S(2)}, u32[]{:S(2)}) async-start(bf16[16,128,128]{2,1,0:T(8,128)(2,1)} %in_grad.1), calls=%async_computation | async-start | bytes 1048576 | tf_op jit(solution)/shard_map/all_to_all | solution.py:246
  61.4 5.3 %collective-permute-start.3 = (f32[8,128]{1,0:T(8,128)S(1)}, f32[8,128]{1,0:T(8,128)S(1)}, u32[]{:S(2)}, u32[]{:S(2)}) collective-permute-start(f32[8,128]{1,0:T(8,128)S(1)} %reduce_sum.19), channel_id=1, source_target_pairs={{0,16},{16,0},{1,17},{17,1},{2,18},{18,2},{3,19},{19,3},{4,20},{20... | collective-permute-start | bytes 12296 | tf_op jit(solution)/shard_map/ppermute | solution.py:248
  66.7 5.0 %collective-permute-done.3 = f32[8,128]{1,0:T(8,128)S(1)} collective-permute-done((f32[8,128]{1,0:T(8,128)S(1)}, f32[8,128]{1,0:T(8,128)S(1)}, u32[]{:S(2)}, u32[]{:S(2)}) %collective-permute-start.3) | collective-permute-done | bytes 4128 | tf_op jit(solution)/shard_map/ppermute | solution.py:248
  71.7 2.5 %collective-permute-start.4 = (f32[8,128]{1,0:T(8,128)S(1)}, f32[8,128]{1,0:T(8,128)S(1)}, u32[]{:S(2)}, u32[]{:S(2)}) collective-permute-start(f32[8,128]{1,0:T(8,128)S(1)} %add.17.mine), channel_id=1, source_target_pairs={{0,8},{8,0},{1,9},{9,1},{2,10},{10,2},{3,11},{11,3},{4,12},{12,4},... | collective-permute-start | bytes 12296 | tf_op jit(solution)/shard_map/ppermute | solution.py:249
  74.2 0.1 pad_add_fusion.place
  74.3 0.7 collective-permute-done.4.theirs
  75.0 1.5 %last.1 = (bf16[128,2048]{1,0:T(8,128)(2,1)}, f32[16,32]{1,0:T(8,128)}) custom-call(s32[2]{0:T(128)S(1)} %pad_add_fusion.place, bf16[16,128,128]{2,1,0:T(8,128)(2,1)S(1)} %all-to-all-done.got, f32[8,128]{1,0:T(8,128)S(1)} %add.17.mine, f32[8,128]{1,0:T(8,128)S(1)} %collective-permute-done.4.theirs), custom_call_target="tpu_custom_call" | custom-call | tf_op jit(solution)/shard_map/last/pallas_call | solution.py:252
  (13 shorter events, 0.1 us)
Async XLA Ops:
  0.6 41.7 %copy-start = (bf16[16,2048]{1,0:T(8,128)(2,1)S(1)}, bf16[16,2048]{1,0:T(8,128)(2,1)}, u32[]{:S(2)}) copy-start(bf16[16,2048]{1,0:T(8,128)(2,1)} %param.6) | copy-start | bytes 196612
  0.7 1.1 %copy-start.1 = (bf16[1024,256]{1,0:T(8,128)(2,1)S(1)}, bf16[1024,256]{1,0:T(8,128)(2,1)}, u32[]{:S(2)}) copy-start(bf16[1024,256]{1,0:T(8,128)(2,1)} %dy.1) | copy-start | bytes 1572868
  1.7 1.0 %copy-start.2 = (bf16[1024,256]{1,0:T(8,128)(2,1)S(1)}, bf16[1024,256]{1,0:T(8,128)(2,1)}, u32[]{:S(2)}) copy-start(bf16[1024,256]{1,0:T(8,128)(2,1)} %x.1) | copy-start | bytes 1572868
  2.9 11.4 %copy-start.3 = (s32[16,16]{1,0:T(8,128)S(1)}, s32[16,16]{1,0:T(8,128)}, u32[]{:S(2)}) copy-start(s32[16,16]{1,0:T(8,128)} %param.7) | copy-start | bytes 3076
  2.9 11.6 %collective-permute-start = (bf16[2048,128]{1,0:T(8,128)(2,1)S(1)}, bf16[2048,128]{1,0:T(8,128)(2,1)S(1)}, u32[]{:S(2)}, u32[]{:S(2)}) collective-permute-start(bf16[2048,128]{1,0:T(8,128)(2,1)S(1)} %get-tuple-element.13), channel_id=1, source_target_pairs={{0,8},{8,0},{1,9},{9,1},{2,10},{10,2},{3,11},{11,3},{4,12},{12,4},... | collective-permute-start | bytes 1572872 | tf_op jit(solution)/shard_map/ppermute | solution.py:220
  11.7 11.3 %collective-permute-start.1 = (bf16[1024,128]{1,0:T(8,128)(2,1)S(1)}, bf16[1024,128]{1,0:T(8,128)(2,1)S(1)}, u32[]{:S(2)}, u32[]{:S(2)}) collective-permute-start(bf16[1024,128]{1,0:T(8,128)(2,1)S(1)} %get-tuple-element.10.dy_own), channel_id=1, source_target_pairs={{16,0},{24,8},{32,16},{40,24},{48,32},{56,40},{64,48},{72,56},{80,... | collective-permute-start | bytes 786440 | tf_op jit(solution)/shard_map/ppermute | solution.py:203
  13.0 15.7 %collective-permute-start.2 = (bf16[1024,128]{1,0:T(8,128)(2,1)S(1)}, bf16[1024,128]{1,0:T(8,128)(2,1)S(1)}, u32[]{:S(2)}, u32[]{:S(2)}) collective-permute-start(bf16[1024,128]{1,0:T(8,128)(2,1)S(1)} %get-tuple-element.11.dy_theirs), channel_id=1, source_target_pairs={{16,8},{24,0},{32,24},{40,16},{48,40},{56,32},{64,56},{72,48},{80,... | collective-permute-start | bytes 786440 | tf_op jit(solution)/shard_map/ppermute | solution.py:203
  32.7 21.1 %all-to-all-start.1 = ((f32[16,8,128]{2,1,0:T(8,128)}), f32[16,8,128]{2,1,0:T(8,128)S(1)}, u32[]{:S(2)}, u32[]{:S(2)}) async-start(f32[16,8,128]{2,1,0:T(8,128)} %get-tuple-element.17), calls=%async_computation.1 | async-start | bytes 131072 | tf_op jit(solution)/shard_map/all_to_all | solution.py:245
  53.9 21.1 %all-to-all-start = ((bf16[16,128,128]{2,1,0:T(8,128)(2,1)}), bf16[16,128,128]{2,1,0:T(8,128)(2,1)S(1)}, u32[]{:S(2)}, u32[]{:S(2)}) async-start(bf16[16,128,128]{2,1,0:T(8,128)(2,1)} %in_grad.1), calls=%async_computation | async-start | bytes 1048576 | tf_op jit(solution)/shard_map/all_to_all | solution.py:246
  61.4 10.3 %collective-permute-start.3 = (f32[8,128]{1,0:T(8,128)S(1)}, f32[8,128]{1,0:T(8,128)S(1)}, u32[]{:S(2)}, u32[]{:S(2)}) collective-permute-start(f32[8,128]{1,0:T(8,128)S(1)} %reduce_sum.19), channel_id=1, source_target_pairs={{0,16},{16,0},{1,17},{17,1},{2,18},{18,2},{3,19},{19,3},{4,20},{20... | collective-permute-start | bytes 12296 | tf_op jit(solution)/shard_map/ppermute | solution.py:248
  71.7 3.3 %collective-permute-start.4 = (f32[8,128]{1,0:T(8,128)S(1)}, f32[8,128]{1,0:T(8,128)S(1)}, u32[]{:S(2)}, u32[]{:S(2)}) collective-permute-start(f32[8,128]{1,0:T(8,128)S(1)} %add.17.mine), channel_id=1, source_target_pairs={{0,8},{8,0},{1,9},{9,1},{2,10},{10,2},{3,11},{11,3},{4,12},{12,4},... | collective-permute-start | bytes 12296 | tf_op jit(solution)/shard_map/ppermute | solution.py:249

commit v4 on v3

--- a/solution.py
+++ b/solution.py
@@ -17,7 +17,6 @@
 BF16 = jnp.bfloat16
 F32 = jnp.float32
 VMEM = pl.BlockSpec(memory_space=pltpu.VMEM)
-HBM = pl.BlockSpec(memory_space=pltpu.HBM)
 SMEM = pl.BlockSpec(memory_space=pltpu.SMEM)
 PARAMS = pltpu.CompilerParams(vmem_limit_bytes=24 << 20)
 
@@ -30,56 +29,26 @@
     return block.T.reshape(-1, CPG, BLK)
 
 
-def run_copies(sems, *pairs):
-    copies = [pltpu.make_async_copy(src, dst, sems.at[i]) for i, (src, dst) in enumerate(pairs)]
-    for copy in copies:
-        copy.start()
-    for copy in copies:
-        copy.wait()
-
-
-def cut_kernel(core, dy, mine, theirs, sems):
-    h = core[0]
-    run_copies(
-        sems,
-        (dy.at[:, aligned(h * LANES, LANES)], mine),
-        (dy.at[:, aligned((1 - h) * LANES, LANES)], theirs),
-    )
-
-
-def pack_kernel(core, x, dy_theirs, mine, pair, sems):
-    h = core[0]
-    rows = x.shape[0]
-    run_copies(
-        sems,
-        (x.at[:, aligned(h * LANES, LANES)], mine),
-        (dy_theirs, pair.at[:rows]),
-        (x.at[:, aligned((1 - h) * LANES, LANES)], pair.at[rows:]),
-    )
-
-
-def own_kernel(core, dy_own, x_own, pair, dy_out, x_out):
-    per_core = dy_own.shape[0] // BLK
-    h = core[0]
+def turn(core, whole, gathered, out):
+    per_core = whole.shape[0] // BLK
+    mine = aligned(core * LANES, LANES)
+    for i in range(per_core):
+        here = pl.ds(i * BLK, BLK)
+        out[:, aligned((core * per_core + i) * CPG, CPG), :] = transposed(whole[here, mine])
+        other = transposed(gathered[1 - core, here, :])
+        out[:, aligned(((1 - core) * per_core + i) * CPG, CPG), :] = other
+
+
+def own_kernel(core, dy, dy_gathered, x, x_gathered, dy_out, x_out, x_t):
     row = lax.broadcasted_iota(jnp.int32, (BLK, BLK), 0)
     col = lax.broadcasted_iota(jnp.int32, (BLK, BLK), 1)
     flip = jnp.where(row + col == BLK - 1, 1.0, 0.0).astype(BF16)
-
-    def run(x_t):
-        for i in range(per_core):
-            here = pl.ds(i * BLK, BLK)
-            first = aligned((h * per_core + i) * CPG, CPG)
-            second = aligned(((1 - h) * per_core + i) * CPG, CPG)
-            dy_out[:, first, :] = transposed(dy_own[here, :])
-            dy_out[:, second, :] = transposed(pair[here, :])
-            x_t[:, first, :] = transposed(x_own[here, :])
-            x_t[:, second, :] = transposed(pair[pl.ds((per_core + i) * BLK, BLK), :])
-        for g in range(x_t.shape[0]):
-            x_out[g] = lax.dot_general(
-                flip, x_t[g], (((1,), (1,)), ((), ())), preferred_element_type=F32
-            ).astype(BF16)
-
-    pl.run_scoped(run, pltpu.VMEM(dy_out.shape, BF16))
+    turn(core[0], dy, dy_gathered, dy_out)
+    turn(core[0], x, x_gathered, x_t)
+    for g in range(x_t.shape[0]):
+        x_out[g] = lax.dot_general(
+            flip, x_t[g], (((1,), (1,)), ((), ())), preferred_element_type=F32
+        ).astype(BF16)
 
 
 def window(own, later, g, k):
@@ -92,14 +61,9 @@
     return jnp.concatenate([window(own, later, g, k), window(own, later, g, k + 1)], axis=1)
 
 
-def filt_grad_kernel(level, core, x_flip, own, later_same, later_other, send_ref, later, dh_ref):
+def filt_grad_kernel(level, core, x_flip, own, dy, dy_gathered, send_ref, later, dh_ref):
     groups = own.shape[0]
-    per_core = later_same.shape[0] // BLK
-    h = core[0]
-    for i in range(per_core):
-        here = pl.ds(i * BLK, BLK)
-        later[:, aligned((h * per_core + i) * CPG, CPG), :] = transposed(later_same[here, :])
-        later[:, aligned(((1 - h) * per_core + i) * CPG, CPG), :] = transposed(later_other[here, :])
+    turn(core[0], dy, dy_gathered, later)
     row = lax.broadcasted_iota(jnp.int32, (BLK, BLK), 0)
     col = lax.broadcasted_iota(jnp.int32, (BLK, BLK), 1)
     within = row + col >= BLK - 1
@@ -165,17 +129,17 @@
     lax.fori_loop(0, own.shape[0], one_group, 0, unroll=8)
 
 
-def last_kernel(scale, place, got, mine, theirs, wide, narrow):
+def last_kernel(scale, shift, got, parts, wide, narrow):
     cores = 2
     grps = got.shape[0] // cores
+    groups = parts.shape[1]
     for h in range(cores):
         for r in range(grps):
             at = (r * cores + h) * LANES
             wide[:, at : at + LANES] = got[h * grps + r].T
-    core, shift = place[0], place[1]
-    groups = mine.shape[0]
-    for at, part in ((core, mine), (1 - core, theirs)):
-        narrow[aligned(at * groups, groups), :] = pltpu.roll(part[...], shift, 1)[:, :QUART] * scale
+        total = parts[h] + parts[cores + h]
+        lags = pltpu.roll(total, shift[0], 1)[:, :QUART]
+        narrow[h * groups : (h + 1) * groups, :] = lags * scale
 
 
 def call(kernel, name, outs, in_specs, scratch=()):
@@ -198,26 +162,12 @@
     h = lax.axis_index("core")
     seq = ("z", "xh", "core")
 
-    def earlier_chip(block, swap):
-        pairs = [(2 * c + o, 2 * (c - 1) + (o ^ swap)) for c in range(1, chips) for o in range(2)]
-        return lax.ppermute(block, seq, pairs)
-
-    half = jax.ShapeDtypeStruct((rows, LANES), BF16)
-
-    dy_mine, dy_theirs = call(
-        cut_kernel, "cut", (half, half), [SMEM, HBM], [pltpu.SemaphoreType.DMA((2,))]
-    )(h[None], out_grad)
-    later_same = earlier_chip(dy_mine, 0)
-    later_other = earlier_chip(dy_theirs, 1)
-    x_mine, pair = call(
-        pack_kernel,
-        "pack",
-        (half, jax.ShapeDtypeStruct((2 * rows, LANES), BF16)),
-        [SMEM, HBM, VMEM],
-        [pltpu.SemaphoreType.DMA((3,))],
-    )(h[None], inputs, dy_theirs)
-    swap = [(0, 1), (1, 0)]
-    pair = lax.ppermute(pair, "core", swap)
+    def swapped(whole):
+        theirs = lax.dynamic_slice_in_dim(whole, (1 - h) * LANES, LANES, 1)
+        return lax.all_gather(theirs, "core")
+
+    later_dy = lax.ppermute(out_grad, seq, [(i, i - 2) for i in range(2, 2 * chips)])
+
     level = lax.dynamic_slice_in_dim(jnp.sum(band, axis=1), h * groups, groups, 0)
     my_filt = lax.dynamic_slice_in_dim(filt, h * groups, groups, 0)
     turned = my_filt.reshape(groups, NOFF, BLK)[:, :, ::-1].astype(F32)
@@ -226,15 +176,16 @@
         own_kernel,
         "own",
         (turned_shape, jax.ShapeDtypeStruct((groups, BLK, blocks * CPG), BF16)),
-        [SMEM] + [VMEM] * 3,
-    )(h[None], dy_mine, x_mine, pair)
+        [SMEM] + [VMEM] * 4,
+        [pltpu.VMEM(turned_shape.shape, BF16)],
+    )(h[None], out_grad, swapped(out_grad), inputs, swapped(inputs))
     send, later = call(
         filt_grad_kernel,
         "filt_grad",
         (jax.ShapeDtypeStruct((NOFF, groups, LANES), F32), turned_shape),
         [SMEM, SMEM] + [VMEM] * 4,
         [pltpu.VMEM((NOFF, groups, 8, BLK), F32)],
-    )(level, h[None], x_flip, own, later_same, later_other)
+    )(level, h[None], x_flip, own, later_dy, swapped(later_dy))
     dx = call(
         in_grad_kernel,
         "in_grad",
@@ -244,9 +195,7 @@
 
     got = lax.all_to_all(send, "z", 0, 0, tiled=True)
     wide = lax.all_to_all(dx, ("core", "grp"), 0, 0, tiled=True)
-    total = jnp.sum(got, axis=0)
-    total = total + lax.ppermute(total, "xh", swap)
-    theirs = lax.ppermute(total, "core", swap)
+    parts = lax.all_gather(jnp.sum(got, axis=0), ("xh", "core"))
     shift = (LANES - (2 * lax.axis_index("xh") + h) * QUART) % LANES
     scale = 1.0 / math.sqrt(rows * 2 * chips * CPG)
     return call(
@@ -256,8 +205,8 @@
             jax.ShapeDtypeStruct((BLK, blocks * LANES), BF16),
             jax.ShapeDtypeStruct((2 * groups, QUART), F32),
         ),
-        [SMEM] + [VMEM] * 3,
-    )(jnp.stack([h, shift]), wide, total, theirs)
+        [SMEM] + [VMEM] * 2,
+    )(shift[None], wide, parts)
 
 
 def solution(mesh):

time: 77 us -> 72.4 us (0.940)
  blocking collectives: 0 us -> 30 us
  waiting for transfers between devices: 27.1 us -> 7.71 us
  starting transfers between devices: 36.2 us -> 22.9 us
  local copies, waits for them, and re-layouts: 2.19 us -> 1.24 us
    all_gather x0 -> x4, blocking collectives: none -> 30 us  [the longest x3 18.4 us: swapped(): return lax.all_gather(theirs, 'core')]
    ppermute x5 -> x1, waiting for transfers between devices: 19.4 us -> 0.01 us  [per_device(): lax.ppermute(out_grad, seq, [(i, i - 2) for i in range(2, 2 * chips)])]
    ppermute x5 -> x1, starting transfers between devices: 19.1 us -> 1.42 us  [per_device(): lax.ppermute(out_grad, seq, [(i, i - 2) for i in range(2, 2 * chips)])]
    all_to_all x1, starting transfers between devices: 9.54 us -> 14 us  [per_device(): got = lax.all_to_all(send, 'z', 0, 0, tiled=True)]
    unnamed x10, local copies, waits for them, and re-layouts: 2.02 us -> 0.04 us
    dynamic_slice x0 -> x3, local copies, waits for them, and re-layouts: none -> 1.02 us  [swapped(): theirs = lax.dynamic_slice_in_dim(whole, (1 - h) * LANES, LANES, 1)]
  transfers between devices with their start and end apart: 7 -> 3, of which waited for: 5 -> 1; matrix products, arithmetic and copies ran while one was open for 1% -> 2% of each run, Pallas kernels for 6% -> 6%
where the time goes in v4:
time: 72.4 us; the launch traced here: 72 us
  blocking collectives  30 us (41%)
  starting transfers between devices  22.9 us (32%)
  Pallas kernels  9.35 us (13%)
  waiting for transfers between devices  7.71 us (11%)
  local copies, waits for them, and re-layouts  1.24 us (2%)
  between operations  0.76 us (1%)
    all_gather x3, blocking collectives, swapped(): return lax.all_gather(theirs, 'core')  18.4 us
    all_to_all x1, starting transfers between devices, per_device(): got = lax.all_to_all(send, 'z', 0, 0, tiled=True)  14 us
    all_gather x1, blocking collectives, per_device(): parts = lax.all_gather(jnp.sum(got, axis=0), ('xh', 'core'))  11.6 us
    all_to_all x1, waiting for transfers between devices, per_device(): got = lax.all_to_all(send, 'z', 0, 0, tiled=True)  7.71 us
    all_to_all x1, starting transfers between devices, per_device(): wide = lax.all_to_all(dx, ('core', 'grp'), 0, 0, tiled=True)  7.41 us
    pallas_call x1, Pallas kernels, per_device(): call(filt_grad_kernel, 'filt_grad', (jax.ShapeDtypeStruct((NOFF, groups,...  4.01 us
    pallas_call x1, Pallas kernels, per_device(): call(in_grad_kernel, 'in_grad', jax.ShapeDtypeStruct((blocks, LANES, BLK)...  3.83 us
  transfers between devices with their start and end apart: 3, of which 1 were waited for; matrix products, arithmetic and copies ran while one was open for 2% of the time, Pallas kernels for 6%

profile of v4, /device:TPU:1, one launch (start us, length us, event | category | flops | bytes accessed | tf_op | source)
XLA Modules:
  0.0 72.0 jit_solution(16168173084618851693)
XLA Ops:
  0.6 0.0 copy-start
  0.6 0.0 copy-start.3
  0.7 0.0 copy-start.1
  0.7 1.4 %collective-permute-start = (bf16[1024,256]{1,0:T(8,128)(2,1)}, bf16[1024,256]{1,0:T(8,128)(2,1)S(1)}, u32[]{:S(2)}, u32[]{:S(2)}) collective-permute-start(bf16[1024,256]{1,0:T(8,128)(2,1)} %dy.1), channel_id=1, source_target_pairs={{16,0},{24,8},{32,16},{40,24},{48,32},{56,40},{64,48},{72,56},{80,... | collective-permute-start | bytes 1572872 | tf_op jit(solution)/shard_map/ppermute | solution.py:169
  2.1 0.0 copy-done.3
  2.1 0.1 reduce_sum.18
  2.2 0.1 dynamic_slice.15.level
  2.3 1.0 %constant_dynamic-slice_fusion.2 = bf16[1024,128]{1,0:T(8,128)(2,1)S(1)} fusion(bf16[1024,256]{1,0:T(8,128)(2,1)} %dy.1, s32[]{:T(128)S(6)} %select_n.18), kind=kLoop, calls=%fused_computation.4 | loop fusion | bytes 524292 | tf_op jit(solution)/shard_map/dynamic_slice | solution.py:166
  3.3 8.7 %all-gather = bf16[2048,128]{1,0:T(8,128)(2,1)S(1)} all-gather(bf16[1024,128]{1,0:T(8,128)(2,1)S(1)} %constant_dynamic-slice_fusion.2), channel_id=2, replica_groups=mesh['z'=16,'xh'=2,'core'=2,'grp'=8] {'core'}, dimensions={0}, use_global_device_ids=true | all-gather | bytes 786432 | tf_op jit(solution)/shard_map/all_gather | solution.py:167
  12.0 2.3 %all-gather.1 = bf16[2048,128]{1,0:T(8,128)(2,1)S(1)} all-gather(bf16[1024,128]{1,0:T(8,128)(2,1)S(1)} %constant_dynamic-slice_fusion.1), channel_id=3, replica_groups=mesh['z'=16,'xh'=2,'core'=2,'grp'=8] {'core'}, dimensions={0}, use_global_device_ids=true | all-gather | bytes 786432 | tf_op jit(solution)/shard_map/all_gather | solution.py:167
  14.3 0.0 copy-done.2
  14.3 0.5 own.1
  14.8 0.0 collective-permute-done.dy
  14.9 7.4 %all-gather.2 = bf16[2048,128]{1,0:T(8,128)(2,1)S(1)} all-gather(bf16[1024,128]{1,0:T(8,128)(2,1)S(1)} %constant_dynamic-slice_fusion), channel_id=4, replica_groups=mesh['z'=16,'xh'=2,'core'=2,'grp'=8] {'core'}, dimensions={0}, use_global_device_ids=true | all-gather | bytes 786432 | tf_op jit(solution)/shard_map/all_gather | solution.py:167
  22.3 4.0 %filt_grad.1 = (f32[16,8,128]{2,1,0:T(8,128)}, bf16[8,256,128]{2,1,0:T(8,128)(2,1)S(1)}) custom-call(s32[8]{0:T(128)S(1)} %dynamic_slice.15.level, s32[1]{0:T(128)} %bitcast.1.core, bf16[8,128,256]{2,1,0:T(8,128)(2,1)S(1)} %get-tuple-element.7.x_flip, bf16[8,256,128]{2,1,0:T(8,128)(2,1)S(1)} %get-tuple-element.6.own, ...), custom_call_target="tpu_custom_call" | custom-call | tf_op jit(solution)/shard_map/filt_grad/pallas_call | solution.py:182
  26.3 14.0 %all-to-all-start.1 = ((f32[16,8,128]{2,1,0:T(8,128)}), f32[16,8,128]{2,1,0:T(8,128)S(1)}, u32[]{:S(2)}, u32[]{:S(2)}) async-start(f32[16,8,128]{2,1,0:T(8,128)} %get-tuple-element.9), calls=%async_computation.1 | async-start | bytes 131072 | tf_op jit(solution)/shard_map/all_to_all | solution.py:196
  40.3 0.0 copy-done
  40.4 0.1 rev.3
  40.5 3.8 %in_grad.1 = bf16[16,128,128]{2,1,0:T(8,128)(2,1)} custom-call(s32[8]{0:T(128)S(1)} %dynamic_slice.15.level, f32[8,16,128]{2,1,0:T(8,128)S(1)} %convert_element_type.3.turned_filt, bf16[8,256,128]{2,1,0:T(8,128)(2,1)S(1)} %get-tuple-element.6.own, bf16[8,256,128]{2,1,0:T(8,128)(2,1)S(1)} %get-tuple-element.8.later), custom_call_target="tpu_custom_call" | custom-call | tf_op jit(solution)/shard_map/in_grad/pallas_call | solution.py:189
  44.3 7.7 %all-to-all-done.1 = f32[16,8,128]{2,1,0:T(8,128)S(1)} async-done(((f32[16,8,128]{2,1,0:T(8,128)}), f32[16,8,128]{2,1,0:T(8,128)S(1)}, u32[]{:S(2)}, u32[]{:S(2)}) %all-to-all-start.1) | async-done | bytes 65568 | tf_op jit(solution)/shard_map/all_to_all | solution.py:196
  52.0 7.4 %all-to-all-start = ((bf16[16,128,128]{2,1,0:T(8,128)(2,1)}), bf16[16,128,128]{2,1,0:T(8,128)(2,1)S(1)}, u32[]{:S(2)}, u32[]{:S(2)}) async-start(bf16[16,128,128]{2,1,0:T(8,128)(2,1)} %in_grad.1), calls=%async_computation | async-start | bytes 1048576 | tf_op jit(solution)/shard_map/all_to_all | solution.py:197
  59.5 11.6 %all-gather.3 = f32[32,128]{1,0:T(8,128)S(1)} all-gather(f32[8,128]{1,0:T(8,128)S(1)} %reduce_sum.19), channel_id=5, replica_groups=mesh['z'=16,'xh'=2,'core'=2,'grp'=8] {'xh','core'}, dimensions={0}, use_global_device_ids=true | all-gather | bytes 20480 | tf_op jit(solution)/shard_map/all_gather | solution.py:198
  71.0 0.0 all-to-all-done.got
  71.0 1.0 %last.1 = (bf16[128,2048]{1,0:T(8,128)(2,1)}, f32[16,32]{1,0:T(8,128)}) custom-call(s32[1]{0:T(128)} %bitcast.shift, bf16[16,128,128]{2,1,0:T(8,128)(2,1)S(1)} %all-to-all-done.got, f32[4,8,128]{2,1,0:T(8,128)S(1)} %bitcast.14), custom_call_target="tpu_custom_call" | custom-call | tf_op jit(solution)/shard_map/last/pallas_call | solution.py:201
  (8 shorter events, 0.1 us)
Async XLA Ops:
  0.6 39.7 %copy-start = (bf16[16,2048]{1,0:T(8,128)(2,1)S(1)}, bf16[16,2048]{1,0:T(8,128)(2,1)}, u32[]{:S(2)}) copy-start(bf16[16,2048]{1,0:T(8,128)(2,1)} %param.6) | copy-start | bytes 196612
  0.6 1.5 %copy-start.3 = (s32[16,16]{1,0:T(8,128)S(1)}, s32[16,16]{1,0:T(8,128)}, u32[]{:S(2)}) copy-start(s32[16,16]{1,0:T(8,128)} %param.7) | copy-start | bytes 3076
  0.7 2.6 %copy-start.1 = (bf16[1024,256]{1,0:T(8,128)(2,1)S(1)}, bf16[1024,256]{1,0:T(8,128)(2,1)}, u32[]{:S(2)}) copy-start(bf16[1024,256]{1,0:T(8,128)(2,1)} %x.1) | copy-start | bytes 1572868
  0.7 14.2 %collective-permute-start = (bf16[1024,256]{1,0:T(8,128)(2,1)}, bf16[1024,256]{1,0:T(8,128)(2,1)S(1)}, u32[]{:S(2)}, u32[]{:S(2)}) collective-permute-start(bf16[1024,256]{1,0:T(8,128)(2,1)} %dy.1), channel_id=1, source_target_pairs={{16,0},{24,8},{32,16},{40,24},{48,32},{56,40},{64,48},{72,56},{80,... | collective-permute-start | bytes 1572872 | tf_op jit(solution)/shard_map/ppermute | solution.py:169
  12.0 2.3 %copy-start.2 = (bf16[1024,256]{1,0:T(8,128)(2,1)S(1)}, bf16[1024,256]{1,0:T(8,128)(2,1)}, u32[]{:S(2)}) copy-start(bf16[1024,256]{1,0:T(8,128)(2,1)} %dy.1) | copy-start | bytes 1572868
  26.3 25.7 %all-to-all-start.1 = ((f32[16,8,128]{2,1,0:T(8,128)}), f32[16,8,128]{2,1,0:T(8,128)S(1)}, u32[]{:S(2)}, u32[]{:S(2)}) async-start(f32[16,8,128]{2,1,0:T(8,128)} %get-tuple-element.9), calls=%async_computation.1 | async-start | bytes 131072 | tf_op jit(solution)/shard_map/all_to_all | solution.py:196
  52.0 19.0 %all-to-all-start = ((bf16[16,128,128]{2,1,0:T(8,128)(2,1)}), bf16[16,128,128]{2,1,0:T(8,128)(2,1)S(1)}, u32[]{:S(2)}, u32[]{:S(2)}) async-start(bf16[16,128,128]{2,1,0:T(8,128)(2,1)} %in_grad.1), calls=%async_computation | async-start | bytes 1048576 | tf_op jit(solution)/shard_map/all_to_all | solution.py:197

commit v5 on v4

--- a/solution.py
+++ b/solution.py
@@ -107,9 +107,10 @@
     return parts[0]
 
 
-def in_grad_kernel(level, turned_filt, own, later, dx_ref):
+def in_grad_kernel(level, core, turned_filt, own, later, mine, theirs):
     row = lax.broadcasted_iota(jnp.int32, (BLK, BLK), 0)
     col = lax.broadcasted_iota(jnp.int32, (BLK, BLK), 1)
+    first = core[0] == 0
 
     def one_group(g, _):
         lags = turned_filt[g]
@@ -123,22 +124,29 @@
             before = here
         wide = jnp.concatenate([window(own, later, g, k) for k in range(NOFF)], axis=1)
         grad = jnp.dot(wide, jnp.concatenate(tiles, axis=0), preferred_element_type=F32)
-        dx_ref[:, aligned(g * CPG, CPG), :] = grad.reshape(-1, CPG, BLK).astype(BF16)
+        blocks = grad.reshape(2, -1, CPG, BLK).astype(BF16)
+        mine[:, aligned(g * CPG, CPG), :] = jnp.where(first, blocks[0], blocks[1])
+        theirs[:, aligned(g * CPG, CPG), :] = jnp.where(first, blocks[1], blocks[0])
         return 0
 
     lax.fori_loop(0, own.shape[0], one_group, 0, unroll=8)
 
 
-def last_kernel(scale, shift, got, parts, wide, narrow):
+def pack_kernel(core, mine, gathered, out):
+    out[:, :LANES, :] = mine[...]
+    out[:, LANES:, :] = gathered[1 - core[0]]
+
+
+def last_kernel(scale, place, got, parts, wide, narrow):
     cores = 2
-    grps = got.shape[0] // cores
     groups = parts.shape[1]
+    for r in range(got.shape[0]):
+        for i, h in enumerate((place[0], 1 - place[0])):
+            at = aligned((r * cores + h) * LANES, LANES)
+            wide[:, at] = got[r, i * LANES : (i + 1) * LANES, :].T
     for h in range(cores):
-        for r in range(grps):
-            at = (r * cores + h) * LANES
-            wide[:, at : at + LANES] = got[h * grps + r].T
         total = parts[h] + parts[cores + h]
-        lags = pltpu.roll(total, shift[0], 1)[:, :QUART]
+        lags = pltpu.roll(total, place[1], 1)[:, :QUART]
         narrow[h * groups : (h + 1) * groups, :] = lags * scale
 
 
@@ -186,15 +194,22 @@
         [SMEM, SMEM] + [VMEM] * 4,
         [pltpu.VMEM((NOFF, groups, 8, BLK), F32)],
     )(level, h[None], x_flip, own, later_dy, swapped(later_dy))
-    dx = call(
+    half = jax.ShapeDtypeStruct((blocks // 2, LANES, BLK), BF16)
+    mine, theirs = call(
         in_grad_kernel,
         "in_grad",
-        jax.ShapeDtypeStruct((blocks, LANES, BLK), BF16),
-        [SMEM] + [VMEM] * 3,
-    )(level, turned, own, later)
+        (half, half),
+        [SMEM] * 2 + [VMEM] * 3,
+    )(level, h[None], turned, own, later)
+    dx = call(
+        pack_kernel,
+        "pack",
+        jax.ShapeDtypeStruct((blocks // 2, 2 * LANES, BLK), BF16),
+        [SMEM] + [VMEM] * 2,
+    )(h[None], mine, lax.all_gather(theirs, "core"))
 
     got = lax.all_to_all(send, "z", 0, 0, tiled=True)
-    wide = lax.all_to_all(dx, ("core", "grp"), 0, 0, tiled=True)
+    wide = lax.all_to_all(dx, "grp", 0, 0, tiled=True)
     parts = lax.all_gather(jnp.sum(got, axis=0), ("xh", "core"))
     shift = (LANES - (2 * lax.axis_index("xh") + h) * QUART) % LANES
     scale = 1.0 / math.sqrt(rows * 2 * chips * CPG)
@@ -206,7 +221,7 @@
             jax.ShapeDtypeStruct((2 * groups, QUART), F32),
         ),
         [SMEM] + [VMEM] * 2,
-    )(shift[None], wide, parts)
+    )(jnp.stack([h, shift]), wide, parts)
 
 
 def solution(mesh):

time: 72.4 us -> 70.8 us (0.978)
  blocking collectives: 30 us -> 32.5 us
  waiting for transfers between devices: 7.71 us -> 5.22 us
  starting transfers between devices: 22.9 us -> 20.6 us
    all_to_all x1, waiting for transfers between devices: 7.71 us -> 5.21 us  [per_device(): got = lax.all_to_all(send, 'z', 0, 0, tiled=True)]
    all_gather x0 -> x1, blocking collectives: none -> 2.46 us  [per_device(): lax.all_gather(theirs, 'core')]
    all_to_all x1, starting transfers between devices: 7.41 us -> 5.12 us  [per_device(): wide = lax.all_to_all(dx, 'grp', 0, 0, tiled=True)]
    pallas_call x1 -> x2, Pallas kernels: 3.83 us -> 3.85 us  [the longest x1 3.02 us: per_device(): call(in_grad_kernel, 'in_grad', (half, half), [SMEM] * 2 + [VMEM] * 3)]
where the time goes in v5:
time: 70.8 us; the launch traced here: 70.4 us
  blocking collectives  32.5 us (46%)
  starting transfers between devices  20.6 us (29%)
  Pallas kernels  9.94 us (14%)
  waiting for transfers between devices  5.22 us (7%)
  local copies, waits for them, and re-layouts  1.24 us (2%)
  between operations  0.77 us (1%)
    all_gather x3, blocking collectives, swapped(): return lax.all_gather(theirs, 'core')  18.4 us
    all_to_all x1, starting transfers between devices, per_device(): got = lax.all_to_all(send, 'z', 0, 0, tiled=True)  14 us
    all_gather x1, blocking collectives, per_device(): parts = lax.all_gather(jnp.sum(got, axis=0), ('xh', 'core'))  11.6 us
    all_to_all x1, waiting for transfers between devices, per_device(): got = lax.all_to_all(send, 'z', 0, 0, tiled=True)  5.21 us
    all_to_all x1, starting transfers between devices, per_device(): wide = lax.all_to_all(dx, 'grp', 0, 0, tiled=True)  5.12 us
    pallas_call x1, Pallas kernels, per_device(): call(filt_grad_kernel, 'filt_grad', (jax.ShapeDtypeStruct((NOFF, groups,...  4.02 us
    pallas_call x1, Pallas kernels, per_device(): call(in_grad_kernel, 'in_grad', (half, half), [SMEM] * 2 + [VMEM] * 3)  3.02 us
    all_gather x1, blocking collectives, per_device(): lax.all_gather(theirs, 'core')  2.46 us
  transfers between devices with their start and end apart: 3, of which 1 were waited for; matrix products, arithmetic and copies ran while one was open for 2% of the time, Pallas kernels for 6%

profile of v5, /device:TPU:1, one launch (start us, length us, event | category | flops | bytes accessed | tf_op | source)
XLA Modules:
  0.0 70.4 jit_solution(3299119646503811044)
XLA Ops:
  0.6 0.0 copy-start
  0.6 0.0 copy-start.3
  0.7 1.4 %collective-permute-start = (bf16[1024,256]{1,0:T(8,128)(2,1)}, bf16[1024,256]{1,0:T(8,128)(2,1)S(1)}, u32[]{:S(2)}, u32[]{:S(2)}) collective-permute-start(bf16[1024,256]{1,0:T(8,128)(2,1)} %dy.1), channel_id=1, source_target_pairs={{16,0},{24,8},{32,16},{40,24},{48,32},{56,40},{64,48},{72,56},{80,... | collective-permute-start | bytes 1572872 | tf_op jit(solution)/shard_map/ppermute | solution.py:177
  2.1 0.1 reduce_sum.18
  2.2 0.1 dynamic_slice.15.level
  2.3 1.0 %constant_dynamic-slice_fusion.2 = bf16[1024,128]{1,0:T(8,128)(2,1)S(1)} fusion(bf16[1024,256]{1,0:T(8,128)(2,1)} %dy.1, s32[]{:T(128)S(6)} %select_n.18), kind=kLoop, calls=%fused_computation.4 | loop fusion | bytes 524292 | tf_op jit(solution)/shard_map/dynamic_slice | solution.py:174
  3.3 8.7 %all-gather = bf16[2048,128]{1,0:T(8,128)(2,1)S(1)} all-gather(bf16[1024,128]{1,0:T(8,128)(2,1)S(1)} %constant_dynamic-slice_fusion.2), channel_id=2, replica_groups=mesh['z'=16,'xh'=2,'core'=2,'grp'=8] {'core'}, dimensions={0}, use_global_device_ids=true | all-gather | bytes 786432 | tf_op jit(solution)/shard_map/all_gather | solution.py:175
  12.0 2.3 %all-gather.1 = bf16[2048,128]{1,0:T(8,128)(2,1)S(1)} all-gather(bf16[1024,128]{1,0:T(8,128)(2,1)S(1)} %constant_dynamic-slice_fusion.1), channel_id=3, replica_groups=mesh['z'=16,'xh'=2,'core'=2,'grp'=8] {'core'}, dimensions={0}, use_global_device_ids=true | all-gather | bytes 786432 | tf_op jit(solution)/shard_map/all_gather | solution.py:175
  14.3 0.0 copy-done.2
  14.3 0.5 own.1
  14.8 0.0 collective-permute-done.dy
  14.9 7.4 %all-gather.2 = bf16[2048,128]{1,0:T(8,128)(2,1)S(1)} all-gather(bf16[1024,128]{1,0:T(8,128)(2,1)S(1)} %constant_dynamic-slice_fusion), channel_id=4, replica_groups=mesh['z'=16,'xh'=2,'core'=2,'grp'=8] {'core'}, dimensions={0}, use_global_device_ids=true | all-gather | bytes 786432 | tf_op jit(solution)/shard_map/all_gather | solution.py:175
  22.3 4.0 %filt_grad.1 = (f32[16,8,128]{2,1,0:T(8,128)}, bf16[8,256,128]{2,1,0:T(8,128)(2,1)S(1)}) custom-call(s32[8]{0:T(128)S(1)} %dynamic_slice.15.level, s32[1]{0:T(128)} %bitcast.core, bf16[8,128,256]{2,1,0:T(8,128)(2,1)S(1)} %get-tuple-element.9.x_flip, bf16[8,256,128]{2,1,0:T(8,128)(2,1)S(1)} %get-tuple-element.8.own, ...), custom_call_target="tpu_custom_call" | custom-call | tf_op jit(solution)/shard_map/filt_grad/pallas_call | solution.py:190
  26.3 14.0 %all-to-all-start.1 = ((f32[16,8,128]{2,1,0:T(8,128)}), f32[16,8,128]{2,1,0:T(8,128)S(1)}, u32[]{:S(2)}, u32[]{:S(2)}) async-start(f32[16,8,128]{2,1,0:T(8,128)} %get-tuple-element.13), calls=%async_computation.1 | async-start | bytes 131072 | tf_op jit(solution)/shard_map/all_to_all | solution.py:211
  40.4 0.1 rev.3
  40.5 3.0 %in_grad.1 = (bf16[8,128,128]{2,1,0:T(8,128)(2,1)S(1)}, bf16[8,128,128]{2,1,0:T(8,128)(2,1)S(1)}) custom-call(s32[8]{0:T(128)S(1)} %dynamic_slice.15.level, s32[1]{0:T(128)} %bitcast.core, f32[8,16,128]{2,1,0:T(8,128)S(1)} %convert_element_type.3.turned_filt, bf16[8,256,128]{2,1,0:T(8,128)(2,1)S(1)} %get-tuple-element.8.own, ...), custom_call_target="tpu_custom_call" | custom-call | tf_op jit(solution)/shard_map/in_grad/pallas_call | solution.py:198
  43.5 2.5 %all-gather.3 = bf16[16,128,128]{2,1,0:T(8,128)(2,1)S(1)} all-gather(bf16[8,128,128]{2,1,0:T(8,128)(2,1)S(1)} %get-tuple-element.12), channel_id=5, replica_groups=mesh['z'=16,'xh'=2,'core'=2,'grp'=8] {'core'}, dimensions={0}, use_global_device_ids=true | all-gather | bytes 786432 | tf_op jit(solution)/shard_map/all_gather | solution.py:209
  46.0 0.8 %pack.1 = bf16[8,256,128]{2,1,0:T(8,128)(2,1)} custom-call(s32[1]{0:T(128)} %bitcast.core, bf16[8,128,128]{2,1,0:T(8,128)(2,1)S(1)} %get-tuple-element.11.mine, bf16[2,8,128,128]{3,2,1,0:T(8,128)(2,1)S(1)} %bitcast.14), custom_call_target="tpu_custom_call" | custom-call | tf_op jit(solution)/shard_map/pack/pallas_call | solution.py:204
  46.8 5.2 %all-to-all-done.1 = f32[16,8,128]{2,1,0:T(8,128)S(1)} async-done(((f32[16,8,128]{2,1,0:T(8,128)}), f32[16,8,128]{2,1,0:T(8,128)S(1)}, u32[]{:S(2)}, u32[]{:S(2)}) %all-to-all-start.1) | async-done | bytes 65568 | tf_op jit(solution)/shard_map/all_to_all | solution.py:211
  52.0 5.1 %all-to-all-start = ((bf16[8,256,128]{2,1,0:T(8,128)(2,1)}), bf16[8,256,128]{2,1,0:T(8,128)(2,1)S(1)}, u32[]{:S(2)}, u32[]{:S(2)}) async-start(bf16[8,256,128]{2,1,0:T(8,128)(2,1)} %pack.1), calls=%async_computation | async-start | bytes 1048576 | tf_op jit(solution)/shard_map/all_to_all | solution.py:212
  57.2 0.1 pad_add_fusion.place
  57.3 11.6 %all-gather.4 = f32[32,128]{1,0:T(8,128)S(1)} all-gather(f32[8,128]{1,0:T(8,128)S(1)} %reduce_sum.19), channel_id=6, replica_groups=mesh['z'=16,'xh'=2,'core'=2,'grp'=8] {'xh','core'}, dimensions={0}, use_global_device_ids=true | all-gather | bytes 20480 | tf_op jit(solution)/shard_map/all_gather | solution.py:213
  68.9 0.0 all-to-all-done.got
  68.9 1.6 %last.1 = (bf16[128,2048]{1,0:T(8,128)(2,1)}, f32[16,32]{1,0:T(8,128)}) custom-call(s32[2]{0:T(128)S(1)} %pad_add_fusion.place, bf16[8,256,128]{2,1,0:T(8,128)(2,1)S(1)} %all-to-all-done.got, f32[4,8,128]{2,1,0:T(8,128)S(1)} %bitcast.16), custom_call_target="tpu_custom_call" | custom-call | tf_op jit(solution)/shard_map/last/pallas_call | solution.py:216
  (11 shorter events, 0.1 us)
Async XLA Ops:
  0.6 39.7 %copy-start = (bf16[16,2048]{1,0:T(8,128)(2,1)S(1)}, bf16[16,2048]{1,0:T(8,128)(2,1)}, u32[]{:S(2)}) copy-start(bf16[16,2048]{1,0:T(8,128)(2,1)} %param.6) | copy-start | bytes 196612
  0.6 1.5 %copy-start.3 = (s32[16,16]{1,0:T(8,128)S(1)}, s32[16,16]{1,0:T(8,128)}, u32[]{:S(2)}) copy-start(s32[16,16]{1,0:T(8,128)} %param.7) | copy-start | bytes 3076
  0.7 2.6 %copy-start.1 = (bf16[1024,256]{1,0:T(8,128)(2,1)S(1)}, bf16[1024,256]{1,0:T(8,128)(2,1)}, u32[]{:S(2)}) copy-start(bf16[1024,256]{1,0:T(8,128)(2,1)} %x.1) | copy-start | bytes 1572868
  0.7 14.2 %collective-permute-start = (bf16[1024,256]{1,0:T(8,128)(2,1)}, bf16[1024,256]{1,0:T(8,128)(2,1)S(1)}, u32[]{:S(2)}, u32[]{:S(2)}) collective-permute-start(bf16[1024,256]{1,0:T(8,128)(2,1)} %dy.1), channel_id=1, source_target_pairs={{16,0},{24,8},{32,16},{40,24},{48,32},{56,40},{64,48},{72,56},{80,... | collective-permute-start | bytes 1572872 | tf_op jit(solution)/shard_map/ppermute | solution.py:177
  12.0 2.3 %copy-start.2 = (bf16[1024,256]{1,0:T(8,128)(2,1)S(1)}, bf16[1024,256]{1,0:T(8,128)(2,1)}, u32[]{:S(2)}) copy-start(bf16[1024,256]{1,0:T(8,128)(2,1)} %dy.1) | copy-start | bytes 1572868
  26.3 25.7 %all-to-all-start.1 = ((f32[16,8,128]{2,1,0:T(8,128)}), f32[16,8,128]{2,1,0:T(8,128)S(1)}, u32[]{:S(2)}, u32[]{:S(2)}) async-start(f32[16,8,128]{2,1,0:T(8,128)} %get-tuple-element.13), calls=%async_computation.1 | async-start | bytes 131072 | tf_op jit(solution)/shard_map/all_to_all | solution.py:211
  52.0 16.8 %all-to-all-start = ((bf16[8,256,128]{2,1,0:T(8,128)(2,1)}), bf16[8,256,128]{2,1,0:T(8,128)(2,1)S(1)}, u32[]{:S(2)}, u32[]{:S(2)}) async-start(bf16[8,256,128]{2,1,0:T(8,128)(2,1)} %pack.1), calls=%async_computation | async-start | bytes 1048576 | tf_op jit(solution)/shard_map/all_to_all | solution.py:212

commit v6 on v5

--- a/solution.py
+++ b/solution.py
@@ -61,7 +61,7 @@
     return jnp.concatenate([window(own, later, g, k), window(own, later, g, k + 1)], axis=1)
 
 
-def filt_grad_kernel(level, core, x_flip, own, dy, dy_gathered, send_ref, later, dh_ref):
+def filt_grad_kernel(core, level, x_flip, own, dy, dy_gathered, send_ref, later, dh_ref):
     groups = own.shape[0]
     turn(core[0], dy, dy_gathered, later)
     row = lax.broadcasted_iota(jnp.int32, (BLK, BLK), 0)
@@ -69,7 +69,7 @@
     within = row + col >= BLK - 1
 
     for g in range(groups):
-        count = level[g]
+        count = level[g : g + 1, :]
 
         def diagonals(k, now, after):
             after = 0.0 if after is None else jnp.where(k + 1 < count, after, 0.0)
@@ -107,20 +107,21 @@
     return parts[0]
 
 
-def in_grad_kernel(level, core, turned_filt, own, later, mine, theirs):
+def in_grad_kernel(core, level, turned_filt, own, later, mine, theirs):
     row = lax.broadcasted_iota(jnp.int32, (BLK, BLK), 0)
     col = lax.broadcasted_iota(jnp.int32, (BLK, BLK), 1)
     first = core[0] == 0
 
     def one_group(g, _):
         lags = turned_filt[g]
+        count = level[pl.ds(g, 1), :]
         before = jnp.zeros((BLK, BLK), F32)
         tiles = []
         for k in range(NOFF):
             spread = jnp.broadcast_to(lags[k : k + 1], (BLK, BLK))
             here = pltpu.roll(spread, 1, 1, stride=1, stride_axis=0)
             tile = jnp.where(col > row, before, here)
-            tiles.append(jnp.where(k < level[g], tile, 0.0).astype(BF16))
+            tiles.append(jnp.where(k < count, tile, 0.0).astype(BF16))
             before = here
         wide = jnp.concatenate([window(own, later, g, k) for k in range(NOFF)], axis=1)
         grad = jnp.dot(wide, jnp.concatenate(tiles, axis=0), preferred_element_type=F32)
@@ -137,16 +138,19 @@
     out[:, LANES:, :] = gathered[1 - core[0]]
 
 
-def last_kernel(scale, place, got, parts, wide, narrow):
+def last_kernel(scale, core, shift, got, parts, wide, narrow):
     cores = 2
     groups = parts.shape[1]
+    first = core[0] == 0
     for r in range(got.shape[0]):
-        for i, h in enumerate((place[0], 1 - place[0])):
-            at = aligned((r * cores + h) * LANES, LANES)
-            wide[:, at] = got[r, i * LANES : (i + 1) * LANES, :].T
+        mine = got[r, :LANES, :].T
+        other = got[r, LANES:, :].T
+        at = r * cores * LANES
+        wide[:, at : at + LANES] = jnp.where(first, mine, other)
+        wide[:, at + LANES : at + 2 * LANES] = jnp.where(first, other, mine)
     for h in range(cores):
         total = parts[h] + parts[cores + h]
-        lags = pltpu.roll(total, place[1], 1)[:, :QUART]
+        lags = pltpu.roll(total, shift[0], 1)[:, :QUART]
         narrow[h * groups : (h + 1) * groups, :] = lags * scale
 
 
@@ -176,7 +180,8 @@
 
     later_dy = lax.ppermute(out_grad, seq, [(i, i - 2) for i in range(2, 2 * chips)])
 
-    level = lax.dynamic_slice_in_dim(jnp.sum(band, axis=1), h * groups, groups, 0)
+    level = lax.dynamic_slice_in_dim(jnp.sum(band, axis=1, keepdims=True), h * groups, groups, 0)
+    level = jnp.broadcast_to(level, (groups, BLK))
     my_filt = lax.dynamic_slice_in_dim(filt, h * groups, groups, 0)
     turned = my_filt.reshape(groups, NOFF, BLK)[:, :, ::-1].astype(F32)
     turned_shape = jax.ShapeDtypeStruct((groups, blocks * CPG, BLK), BF16)
@@ -191,16 +196,16 @@
         filt_grad_kernel,
         "filt_grad",
         (jax.ShapeDtypeStruct((NOFF, groups, LANES), F32), turned_shape),
-        [SMEM, SMEM] + [VMEM] * 4,
+        [SMEM] + [VMEM] * 5,
         [pltpu.VMEM((NOFF, groups, 8, BLK), F32)],
-    )(level, h[None], x_flip, own, later_dy, swapped(later_dy))
+    )(h[None], level, x_flip, own, later_dy, swapped(later_dy))
     half = jax.ShapeDtypeStruct((blocks // 2, LANES, BLK), BF16)
     mine, theirs = call(
         in_grad_kernel,
         "in_grad",
         (half, half),
-        [SMEM] * 2 + [VMEM] * 3,
-    )(level, h[None], turned, own, later)
+        [SMEM] + [VMEM] * 4,
+    )(h[None], level, turned, own, later)
     dx = call(
         pack_kernel,
         "pack",
@@ -220,8 +225,8 @@
             jax.ShapeDtypeStruct((BLK, blocks * LANES), BF16),
             jax.ShapeDtypeStruct((2 * groups, QUART), F32),
         ),
-        [SMEM] + [VMEM] * 2,
-    )(jnp.stack([h, shift]), wide, parts)
+        [SMEM] * 2 + [VMEM] * 2,
+    )(h[None], shift[None], wide, parts)
 
 
 def solution(mesh):

time: 70.8 us -> 69.8 us (0.986)
  Pallas kernels: 9.94 us -> 8.31 us
where the time goes in v6:
time: 69.8 us; the launch traced here: 69.4 us
  blocking collectives  32.6 us (47%)
  starting transfers between devices  20.6 us (30%)
  Pallas kernels  8.31 us (12%)
  waiting for transfers between devices  5.75 us (8%)
  local copies, waits for them, and re-layouts  1.3 us (2%)
  between operations  0.77 us (1%)
    all_gather x3, blocking collectives, swapped(): return lax.all_gather(theirs, 'core')  18.4 us
    all_to_all x1, starting transfers between devices, per_device(): got = lax.all_to_all(send, 'z', 0, 0, tiled=True)  14 us
    all_gather x1, blocking collectives, per_device(): parts = lax.all_gather(jnp.sum(got, axis=0), ('xh', 'core'))  11.7 us
    all_to_all x1, waiting for transfers between devices, per_device(): got = lax.all_to_all(send, 'z', 0, 0, tiled=True)  5.74 us
    all_to_all x1, starting transfers between devices, per_device(): wide = lax.all_to_all(dx, 'grp', 0, 0, tiled=True)  5.12 us
    pallas_call x1, Pallas kernels, per_device(): call(filt_grad_kernel, 'filt_grad', (jax.ShapeDtypeStruct((NOFF, groups,...  3.48 us
    pallas_call x1, Pallas kernels, per_device(): call(in_grad_kernel, 'in_grad', (half, half), [SMEM] + [VMEM] * 4)  2.49 us
    all_gather x1, blocking collectives, per_device(): lax.all_gather(theirs, 'core')  2.46 us
  transfers between devices with their start and end apart: 3, of which 1 were waited for; matrix products, arithmetic and copies ran while one was open for 2% of the time, Pallas kernels for 6%

profile of v6, /device:TPU:1, one launch (start us, length us, event | category | flops | bytes accessed | tf_op | source)
XLA Modules:
  0.0 69.4 jit_solution(18058190703246237490)
XLA Ops:
  0.6 0.0 copy-start
  0.6 0.0 copy-start.3
  0.7 1.4 %collective-permute-start = (bf16[1024,256]{1,0:T(8,128)(2,1)}, bf16[1024,256]{1,0:T(8,128)(2,1)S(1)}, u32[]{:S(2)}, u32[]{:S(2)}) collective-permute-start(bf16[1024,256]{1,0:T(8,128)(2,1)} %dy.1), channel_id=1, source_target_pairs={{16,0},{24,8},{32,16},{40,24},{48,32},{56,40},{64,48},{72,56},{80,... | collective-permute-start | bytes 1572872 | tf_op jit(solution)/shard_map/ppermute | solution.py:181
  2.1 0.1 reduce_sum.18
  2.2 0.1 dynamic-slice.3
  2.3 1.0 %constant_dynamic-slice_fusion.2 = bf16[1024,128]{1,0:T(8,128)(2,1)S(1)} fusion(bf16[1024,256]{1,0:T(8,128)(2,1)} %dy.1, s32[]{:T(128)S(6)} %select_n.18), kind=kLoop, calls=%fused_computation.4 | loop fusion | bytes 524292 | tf_op jit(solution)/shard_map/dynamic_slice | solution.py:178
  3.3 8.7 %all-gather = bf16[2048,128]{1,0:T(8,128)(2,1)S(1)} all-gather(bf16[1024,128]{1,0:T(8,128)(2,1)S(1)} %constant_dynamic-slice_fusion.2), channel_id=2, replica_groups=mesh['z'=16,'xh'=2,'core'=2,'grp'=8] {'core'}, dimensions={0}, use_global_device_ids=true | all-gather | bytes 786432 | tf_op jit(solution)/shard_map/all_gather | solution.py:179
  12.0 2.3 %all-gather.1 = bf16[2048,128]{1,0:T(8,128)(2,1)S(1)} all-gather(bf16[1024,128]{1,0:T(8,128)(2,1)S(1)} %constant_dynamic-slice_fusion.1), channel_id=3, replica_groups=mesh['z'=16,'xh'=2,'core'=2,'grp'=8] {'core'}, dimensions={0}, use_global_device_ids=true | all-gather | bytes 786432 | tf_op jit(solution)/shard_map/all_gather | solution.py:179
  14.3 0.0 copy-done.2
  14.3 0.5 own.1
  14.8 0.0 collective-permute-done.dy
  14.9 7.4 %all-gather.2 = bf16[2048,128]{1,0:T(8,128)(2,1)S(1)} all-gather(bf16[1024,128]{1,0:T(8,128)(2,1)S(1)} %constant_dynamic-slice_fusion), channel_id=4, replica_groups=mesh['z'=16,'xh'=2,'core'=2,'grp'=8] {'core'}, dimensions={0}, use_global_device_ids=true | all-gather | bytes 786432 | tf_op jit(solution)/shard_map/all_gather | solution.py:179
  22.3 0.1 broadcast_in_dim.8.level
  22.4 3.5 %filt_grad.1 = (f32[16,8,128]{2,1,0:T(8,128)}, bf16[8,256,128]{2,1,0:T(8,128)(2,1)S(1)}) custom-call(s32[1]{0:T(128)} %bitcast.core, s32[8,128]{1,0:T(8,128)S(1)} %broadcast_in_dim.8.level, bf16[8,128,256]{2,1,0:T(8,128)(2,1)S(1)} %get-tuple-element.9.x_flip, bf16[8,256,128]{2,1,0:T(8,128)(2,1)S(1)} %get-tuple-element.8.own, ...), custom_call_target="tpu_custom_call" | custom-call | tf_op jit(solution)/shard_map/filt_grad/pallas_call | solution.py:195
  25.8 14.0 %all-to-all-start.1 = ((f32[16,8,128]{2,1,0:T(8,128)}), f32[16,8,128]{2,1,0:T(8,128)S(1)}, u32[]{:S(2)}, u32[]{:S(2)}) async-start(f32[16,8,128]{2,1,0:T(8,128)} %get-tuple-element.13), calls=%async_computation.1 | async-start | bytes 131072 | tf_op jit(solution)/shard_map/all_to_all | solution.py:216
  39.9 0.1 rev.3
  40.0 2.5 %in_grad.1 = (bf16[8,128,128]{2,1,0:T(8,128)(2,1)S(1)}, bf16[8,128,128]{2,1,0:T(8,128)(2,1)S(1)}) custom-call(s32[1]{0:T(128)} %bitcast.core, s32[8,128]{1,0:T(8,128)S(1)} %broadcast_in_dim.8.level, f32[8,16,128]{2,1,0:T(8,128)S(1)} %convert_element_type.3.turned_filt, bf16[8,256,128]{2,1,0:T(8,128)(2,1)S(1)} %get-tuple-element.8.own, ...), custom_call_target="tpu_custom_call" | custom-call | tf_op jit(solution)/shard_map/in_grad/pallas_call | solution.py:203
  42.5 2.5 %all-gather.3 = bf16[16,128,128]{2,1,0:T(8,128)(2,1)S(1)} all-gather(bf16[8,128,128]{2,1,0:T(8,128)(2,1)S(1)} %get-tuple-element.12), channel_id=5, replica_groups=mesh['z'=16,'xh'=2,'core'=2,'grp'=8] {'core'}, dimensions={0}, use_global_device_ids=true | all-gather | bytes 786432 | tf_op jit(solution)/shard_map/all_gather | solution.py:214
  45.0 0.8 %pack.1 = bf16[8,256,128]{2,1,0:T(8,128)(2,1)} custom-call(s32[1]{0:T(128)} %bitcast.core, bf16[8,128,128]{2,1,0:T(8,128)(2,1)S(1)} %get-tuple-element.11.mine, bf16[2,8,128,128]{3,2,1,0:T(8,128)(2,1)S(1)} %bitcast.15), custom_call_target="tpu_custom_call" | custom-call | tf_op jit(solution)/shard_map/pack/pallas_call | solution.py:209
  45.8 5.7 %all-to-all-done.1 = f32[16,8,128]{2,1,0:T(8,128)S(1)} async-done(((f32[16,8,128]{2,1,0:T(8,128)}), f32[16,8,128]{2,1,0:T(8,128)S(1)}, u32[]{:S(2)}, u32[]{:S(2)}) %all-to-all-start.1) | async-done | bytes 65568 | tf_op jit(solution)/shard_map/all_to_all | solution.py:216
  51.6 5.1 %all-to-all-start = ((bf16[8,256,128]{2,1,0:T(8,128)(2,1)}), bf16[8,256,128]{2,1,0:T(8,128)(2,1)S(1)}, u32[]{:S(2)}, u32[]{:S(2)}) async-start(bf16[8,256,128]{2,1,0:T(8,128)(2,1)} %pack.1), calls=%async_computation | async-start | bytes 1048576 | tf_op jit(solution)/shard_map/all_to_all | solution.py:217
  56.7 11.7 %all-gather.4 = f32[32,128]{1,0:T(8,128)S(1)} all-gather(f32[8,128]{1,0:T(8,128)S(1)} %reduce_sum.19), channel_id=6, replica_groups=mesh['z'=16,'xh'=2,'core'=2,'grp'=8] {'xh','core'}, dimensions={0}, use_global_device_ids=true | all-gather | bytes 20480 | tf_op jit(solution)/shard_map/all_gather | solution.py:218
  68.4 0.0 all-to-all-done.got
  68.4 1.0 %last.1 = (bf16[128,2048]{1,0:T(8,128)(2,1)}, f32[16,32]{1,0:T(8,128)}) custom-call(s32[1]{0:T(128)} %bitcast.core, s32[1]{0:T(128)} %bitcast.1.shift, bf16[8,256,128]{2,1,0:T(8,128)(2,1)S(1)} %all-to-all-done.got, f32[4,8,128]{2,1,0:T(8,128)S(1)} %bitcast.16), custom_call_target="tpu_custom_call" | custom-call | tf_op jit(solution)/shard_map/last/pallas_call | solution.py:221
  (11 shorter events, 0.1 us)
Async XLA Ops:
  0.6 39.2 %copy-start = (bf16[16,2048]{1,0:T(8,128)(2,1)S(1)}, bf16[16,2048]{1,0:T(8,128)(2,1)}, u32[]{:S(2)}) copy-start(bf16[16,2048]{1,0:T(8,128)(2,1)} %param.6) | copy-start | bytes 196612
  0.6 1.5 %copy-start.3 = (s32[16,16]{1,0:T(8,128)S(1)}, s32[16,16]{1,0:T(8,128)}, u32[]{:S(2)}) copy-start(s32[16,16]{1,0:T(8,128)} %param.7) | copy-start | bytes 3076
  0.7 2.6 %copy-start.1 = (bf16[1024,256]{1,0:T(8,128)(2,1)S(1)}, bf16[1024,256]{1,0:T(8,128)(2,1)}, u32[]{:S(2)}) copy-start(bf16[1024,256]{1,0:T(8,128)(2,1)} %x.1) | copy-start | bytes 1572868
  0.7 14.2 %collective-permute-start = (bf16[1024,256]{1,0:T(8,128)(2,1)}, bf16[1024,256]{1,0:T(8,128)(2,1)S(1)}, u32[]{:S(2)}, u32[]{:S(2)}) collective-permute-start(bf16[1024,256]{1,0:T(8,128)(2,1)} %dy.1), channel_id=1, source_target_pairs={{16,0},{24,8},{32,16},{40,24},{48,32},{56,40},{64,48},{72,56},{80,... | collective-permute-start | bytes 1572872 | tf_op jit(solution)/shard_map/ppermute | solution.py:181
  12.0 2.3 %copy-start.2 = (bf16[1024,256]{1,0:T(8,128)(2,1)S(1)}, bf16[1024,256]{1,0:T(8,128)(2,1)}, u32[]{:S(2)}) copy-start(bf16[1024,256]{1,0:T(8,128)(2,1)} %dy.1) | copy-start | bytes 1572868
  25.8 25.7 %all-to-all-start.1 = ((f32[16,8,128]{2,1,0:T(8,128)}), f32[16,8,128]{2,1,0:T(8,128)S(1)}, u32[]{:S(2)}, u32[]{:S(2)}) async-start(f32[16,8,128]{2,1,0:T(8,128)} %get-tuple-element.13), calls=%async_computation.1 | async-start | bytes 131072 | tf_op jit(solution)/shard_map/all_to_all | solution.py:216
  51.6 16.8 %all-to-all-start = ((bf16[8,256,128]{2,1,0:T(8,128)(2,1)}), bf16[8,256,128]{2,1,0:T(8,128)(2,1)S(1)}, u32[]{:S(2)}, u32[]{:S(2)}) async-start(bf16[8,256,128]{2,1,0:T(8,128)(2,1)} %pack.1), calls=%async_computation | async-start | bytes 1048576 | tf_op jit(solution)/shard_map/all_to_all | solution.py:217

commit v7 on v6

--- a/solution.py
+++ b/solution.py
@@ -31,11 +31,12 @@
 
 def turn(core, whole, gathered, out):
     per_core = whole.shape[0] // BLK
-    mine = aligned(core * LANES, LANES)
+    mine = aligned(core * LANES, LANES) if whole.shape[1] > LANES else slice(None)
     for i in range(per_core):
         here = pl.ds(i * BLK, BLK)
         out[:, aligned((core * per_core + i) * CPG, CPG), :] = transposed(whole[here, mine])
-        other = transposed(gathered[1 - core, here, :])
+        other = gathered[here, :] if len(gathered.shape) == 2 else gathered[1 - core, here, :]
+        other = transposed(other)
         out[:, aligned(((1 - core) * per_core + i) * CPG, CPG), :] = other
 
 
@@ -178,7 +179,12 @@
         theirs = lax.dynamic_slice_in_dim(whole, (1 - h) * LANES, LANES, 1)
         return lax.all_gather(theirs, "core")
 
-    later_dy = lax.ppermute(out_grad, seq, [(i, i - 2) for i in range(2, 2 * chips)])
+    def earlier_chip(block, swap):
+        pairs = [(i, (i ^ swap) - 2) for i in range(2, 2 * chips)]
+        return lax.ppermute(block, seq, pairs)
+
+    later_same = earlier_chip(lax.dynamic_slice_in_dim(out_grad, h * LANES, LANES, 1), 0)
+    later_other = earlier_chip(lax.dynamic_slice_in_dim(out_grad, (1 - h) * LANES, LANES, 1), 1)
 
     level = lax.dynamic_slice_in_dim(jnp.sum(band, axis=1, keepdims=True), h * groups, groups, 0)
     level = jnp.broadcast_to(level, (groups, BLK))
@@ -198,7 +204,7 @@
         (jax.ShapeDtypeStruct((NOFF, groups, LANES), F32), turned_shape),
         [SMEM] + [VMEM] * 5,
         [pltpu.VMEM((NOFF, groups, 8, BLK), F32)],
-    )(h[None], level, x_flip, own, later_dy, swapped(later_dy))
+    )(h[None], level, x_flip, own, later_same, later_other)
     half = jax.ShapeDtypeStruct((blocks // 2, LANES, BLK), BF16)
     mine, theirs = call(
         in_grad_kernel,

time: 69.8 us -> 68.7 us (0.984)
  blocking collectives: 32.6 us -> 25.2 us
  waiting for transfers between devices: 5.75 us -> 11.5 us
  local copies, waits for them, and re-layouts: 1.3 us -> 2.09 us
    all_gather x3 -> x2, blocking collectives: 18.4 us -> 11 us  [swapped(): return lax.all_gather(theirs, 'core')]
    ppermute x1 -> x2, waiting for transfers between devices: 0.01 us -> 5.99 us  [earlier_chip(): return lax.ppermute(block, seq, pairs)]
    all_to_all x1, starting transfers between devices: 14 us -> 12.6 us  [per_device(): got = lax.all_to_all(send, 'z', 0, 0, tiled=True)]
    ppermute x1 -> x2, starting transfers between devices: 1.42 us -> 2.58 us  [earlier_chip(): return lax.ppermute(block, seq, pairs)]
    dynamic_slice x0 -> x1, local copies, waits for them, and re-layouts: none -> 1.13 us  [per_device(): lax.dynamic_slice_in_dim(out_grad, h * LANES, LANES, 1)]
    dynamic_slice x3 -> x1, local copies, waits for them, and re-layouts: 1.02 us -> 0.03 us  [swapped(): theirs = lax.dynamic_slice_in_dim(whole, (1 - h) * LANES, LANES, 1)]
  transfers between devices with their start and end apart: 3 -> 4, of which waited for: 1 -> 2; matrix products, arithmetic and copies ran while one was open for 2% -> 1% of each run, Pallas kernels for 6% -> 6%
where the time goes in v7:
time: 68.7 us; the launch traced here: 68.4 us
  blocking collectives  25.2 us (37%)
  starting transfers between devices  20.3 us (30%)
  waiting for transfers between devices  11.5 us (17%)
  Pallas kernels  8.29 us (12%)
  local copies, waits for them, and re-layouts  2.09 us (3%)
  between operations  0.76 us (1%)
    all_to_all x1, starting transfers between devices, per_device(): got = lax.all_to_all(send, 'z', 0, 0, tiled=True)  12.6 us
    all_gather x1, blocking collectives, per_device(): parts = lax.all_gather(jnp.sum(got, axis=0), ('xh', 'core'))  11.7 us
    all_gather x2, blocking collectives, swapped(): return lax.all_gather(theirs, 'core')  11 us
    ppermute x2, waiting for transfers between devices, earlier_chip(): return lax.ppermute(block, seq, pairs)  5.99 us
    all_to_all x1, waiting for transfers between devices, per_device(): got = lax.all_to_all(send, 'z', 0, 0, tiled=True)  5.51 us
    all_to_all x1, starting transfers between devices, per_device(): wide = lax.all_to_all(dx, 'grp', 0, 0, tiled=True)  5.21 us
    pallas_call x1, Pallas kernels, per_device(): call(filt_grad_kernel, 'filt_grad', (jax.ShapeDtypeStruct((NOFF, groups,...  3.46 us
    ppermute x2, starting transfers between devices, earlier_chip(): return lax.ppermute(block, seq, pairs)  2.58 us
  transfers between devices with their start and end apart: 4, of which 2 were waited for; matrix products, arithmetic and copies ran while one was open for 1% of the time, Pallas kernels for 6%

profile of v7, /device:TPU:1, one launch (start us, length us, event | category | flops | bytes accessed | tf_op | source)
XLA Modules:
  0.0 68.4 jit_solution(5686312012737072184)
XLA Ops:
  0.6 0.0 copy-start
  0.7 1.1 %constant_dynamic-slice_fusion = (bf16[1024,128]{1,0:T(8,128)(2,1)S(1)}, bf16[1024,128]{1,0:T(8,128)(2,1)S(1)}) fusion(bf16[1024,256]{1,0:T(8,128)(2,1)} %dy.1, s32[]{:T(128)S(6)} %select_n.22, s32[]{:T(128)S(6)} %select_n.21), kind=kLoop, calls=%fused_computation.2 | loop fusion | bytes 1048584 | tf_op jit(solution)/shard_map/dynamic_slice | solution.py:186
  1.8 1.3 %collective-permute-start.1 = (bf16[1024,128]{1,0:T(8,128)(2,1)S(1)}, bf16[1024,128]{1,0:T(8,128)(2,1)S(1)}, u32[]{:S(2)}, u32[]{:S(2)}) collective-permute-start(bf16[1024,128]{1,0:T(8,128)(2,1)S(1)} %get-tuple-element.15), channel_id=1, source_target_pairs={{16,8},{24,0},{32,24},{40,16},{48,40},{56,32},{64,56},{72,48},{80,... | collective-permute-start | bytes 786440 | tf_op jit(solution)/shard_map/ppermute | solution.py:184
  3.1 1.3 %collective-permute-start = (bf16[1024,128]{1,0:T(8,128)(2,1)S(1)}, bf16[1024,128]{1,0:T(8,128)(2,1)S(1)}, u32[]{:S(2)}, u32[]{:S(2)}) collective-permute-start(bf16[1024,128]{1,0:T(8,128)(2,1)S(1)} %get-tuple-element.14), channel_id=1, source_target_pairs={{16,0},{24,8},{32,16},{40,24},{48,32},{56,40},{64,48},{72,56},{80,... | collective-permute-start | bytes 786440 | tf_op jit(solution)/shard_map/ppermute | solution.py:184
  4.4 0.0 copy-start.3
  4.5 0.7 copy-done.3
  5.1 0.1 reduce_sum.18
  5.2 0.1 dynamic-slice.3
  5.3 8.7 %all-gather = bf16[2048,128]{1,0:T(8,128)(2,1)S(1)} all-gather(bf16[1024,128]{1,0:T(8,128)(2,1)S(1)} %get-tuple-element.15), channel_id=2, replica_groups=mesh['z'=16,'xh'=2,'core'=2,'grp'=8] {'core'}, dimensions={0}, use_global_device_ids=true | all-gather | bytes 786432 | tf_op jit(solution)/shard_map/all_gather | solution.py:180
  14.0 2.3 %all-gather.1 = bf16[2048,128]{1,0:T(8,128)(2,1)S(1)} all-gather(bf16[1024,128]{1,0:T(8,128)(2,1)S(1)} %constant_dynamic-slice_fusion.1), channel_id=3, replica_groups=mesh['z'=16,'xh'=2,'core'=2,'grp'=8] {'core'}, dimensions={0}, use_global_device_ids=true | all-gather | bytes 786432 | tf_op jit(solution)/shard_map/all_gather | solution.py:180
  16.3 0.5 own.1
  16.8 0.0 collective-permute-done.1.dy_gathered
  16.8 6.0 %collective-permute-done.dy = bf16[1024,128]{1,0:T(8,128)(2,1)S(1)} collective-permute-done((bf16[1024,128]{1,0:T(8,128)(2,1)S(1)}, bf16[1024,128]{1,0:T(8,128)(2,1)S(1)}, u32[]{:S(2)}, u32[]{:S(2)}) %collective-permute-start) | collective-permute-done | bytes 262176 | tf_op jit(solution)/shard_map/ppermute | solution.py:184
  22.8 0.1 broadcast_in_dim.8.level
  22.9 3.5 %filt_grad.1 = (f32[16,8,128]{2,1,0:T(8,128)}, bf16[8,256,128]{2,1,0:T(8,128)(2,1)S(1)}) custom-call(s32[1]{0:T(128)} %bitcast.core, s32[8,128]{1,0:T(8,128)S(1)} %broadcast_in_dim.8.level, bf16[8,128,256]{2,1,0:T(8,128)(2,1)S(1)} %get-tuple-element.9.x_flip, bf16[8,256,128]{2,1,0:T(8,128)(2,1)S(1)} %get-tuple-element.8.own, ...), custom_call_target="tpu_custom_call" | custom-call | tf_op jit(solution)/shard_map/filt_grad/pallas_call | solution.py:201
  26.3 12.6 %all-to-all-start.1 = ((f32[16,8,128]{2,1,0:T(8,128)}), f32[16,8,128]{2,1,0:T(8,128)S(1)}, u32[]{:S(2)}, u32[]{:S(2)}) async-start(f32[16,8,128]{2,1,0:T(8,128)} %get-tuple-element.13), calls=%async_computation.1 | async-start | bytes 131072 | tf_op jit(solution)/shard_map/all_to_all | solution.py:222
  38.9 0.1 rev.3
  39.0 2.5 %in_grad.1 = (bf16[8,128,128]{2,1,0:T(8,128)(2,1)S(1)}, bf16[8,128,128]{2,1,0:T(8,128)(2,1)S(1)}) custom-call(s32[1]{0:T(128)} %bitcast.core, s32[8,128]{1,0:T(8,128)S(1)} %broadcast_in_dim.8.level, f32[8,16,128]{2,1,0:T(8,128)S(1)} %convert_element_type.3.turned_filt, bf16[8,256,128]{2,1,0:T(8,128)(2,1)S(1)} %get-tuple-element.8.own, ...), custom_call_target="tpu_custom_call" | custom-call | tf_op jit(solution)/shard_map/in_grad/pallas_call | solution.py:209
  41.5 2.6 %all-gather.2 = bf16[16,128,128]{2,1,0:T(8,128)(2,1)S(1)} all-gather(bf16[8,128,128]{2,1,0:T(8,128)(2,1)S(1)} %get-tuple-element.12), channel_id=4, replica_groups=mesh['z'=16,'xh'=2,'core'=2,'grp'=8] {'core'}, dimensions={0}, use_global_device_ids=true | all-gather | bytes 786432 | tf_op jit(solution)/shard_map/all_gather | solution.py:220
  44.1 0.8 %pack.1 = bf16[8,256,128]{2,1,0:T(8,128)(2,1)} custom-call(s32[1]{0:T(128)} %bitcast.core, bf16[8,128,128]{2,1,0:T(8,128)(2,1)S(1)} %get-tuple-element.11.mine, bf16[2,8,128,128]{3,2,1,0:T(8,128)(2,1)S(1)} %bitcast.13), custom_call_target="tpu_custom_call" | custom-call | tf_op jit(solution)/shard_map/pack/pallas_call | solution.py:215
  44.9 5.5 %all-to-all-done.1 = f32[16,8,128]{2,1,0:T(8,128)S(1)} async-done(((f32[16,8,128]{2,1,0:T(8,128)}), f32[16,8,128]{2,1,0:T(8,128)S(1)}, u32[]{:S(2)}, u32[]{:S(2)}) %all-to-all-start.1) | async-done | bytes 65568 | tf_op jit(solution)/shard_map/all_to_all | solution.py:222
  50.5 5.2 %all-to-all-start = ((bf16[8,256,128]{2,1,0:T(8,128)(2,1)}), bf16[8,256,128]{2,1,0:T(8,128)(2,1)S(1)}, u32[]{:S(2)}, u32[]{:S(2)}) async-start(bf16[8,256,128]{2,1,0:T(8,128)(2,1)} %pack.1), calls=%async_computation | async-start | bytes 1048576 | tf_op jit(solution)/shard_map/all_to_all | solution.py:223
  55.7 11.7 %all-gather.3 = f32[32,128]{1,0:T(8,128)S(1)} all-gather(f32[8,128]{1,0:T(8,128)S(1)} %reduce_sum.19), channel_id=5, replica_groups=mesh['z'=16,'xh'=2,'core'=2,'grp'=8] {'xh','core'}, dimensions={0}, use_global_device_ids=true | all-gather | bytes 20480 | tf_op jit(solution)/shard_map/all_gather | solution.py:224
  67.3 1.0 %last.1 = (bf16[128,2048]{1,0:T(8,128)(2,1)}, f32[16,32]{1,0:T(8,128)}) custom-call(s32[1]{0:T(128)} %bitcast.core, s32[1]{0:T(128)} %bitcast.1.shift, bf16[8,256,128]{2,1,0:T(8,128)(2,1)S(1)} %all-to-all-done.got, f32[4,8,128]{2,1,0:T(8,128)S(1)} %bitcast.14), custom_call_target="tpu_custom_call" | custom-call | tf_op jit(solution)/shard_map/last/pallas_call | solution.py:227
  (11 shorter events, 0.1 us)
Async XLA Ops:
  0.6 38.3 %copy-start = (bf16[16,2048]{1,0:T(8,128)(2,1)S(1)}, bf16[16,2048]{1,0:T(8,128)(2,1)}, u32[]{:S(2)}) copy-start(bf16[16,2048]{1,0:T(8,128)(2,1)} %param.6) | copy-start | bytes 196612
  0.7 3.7 %copy-start.2 = (bf16[1024,256]{1,0:T(8,128)(2,1)S(1)}, bf16[1024,256]{1,0:T(8,128)(2,1)}, u32[]{:S(2)}) copy-start(bf16[1024,256]{1,0:T(8,128)(2,1)} %x.1) | copy-start | bytes 1572868
  1.8 15.0 %collective-permute-start.1 = (bf16[1024,128]{1,0:T(8,128)(2,1)S(1)}, bf16[1024,128]{1,0:T(8,128)(2,1)S(1)}, u32[]{:S(2)}, u32[]{:S(2)}) collective-permute-start(bf16[1024,128]{1,0:T(8,128)(2,1)S(1)} %get-tuple-element.15), channel_id=1, source_target_pairs={{16,8},{24,0},{32,24},{40,16},{48,40},{56,32},{64,56},{72,48},{80,... | collective-permute-start | bytes 786440 | tf_op jit(solution)/shard_map/ppermute | solution.py:184
  3.1 19.7 %collective-permute-start = (bf16[1024,128]{1,0:T(8,128)(2,1)S(1)}, bf16[1024,128]{1,0:T(8,128)(2,1)S(1)}, u32[]{:S(2)}, u32[]{:S(2)}) collective-permute-start(bf16[1024,128]{1,0:T(8,128)(2,1)S(1)} %get-tuple-element.14), channel_id=1, source_target_pairs={{16,0},{24,8},{32,16},{40,24},{48,32},{56,40},{64,48},{72,56},{80,... | collective-permute-start | bytes 786440 | tf_op jit(solution)/shard_map/ppermute | solution.py:184
  4.4 0.7 %copy-start.3 = (s32[16,16]{1,0:T(8,128)S(1)}, s32[16,16]{1,0:T(8,128)}, u32[]{:S(2)}) copy-start(s32[16,16]{1,0:T(8,128)} %param.7) | copy-start | bytes 3076
  14.0 2.3 %copy-start.1 = (bf16[1024,256]{1,0:T(8,128)(2,1)S(1)}, bf16[1024,256]{1,0:T(8,128)(2,1)}, u32[]{:S(2)}) copy-start(bf16[1024,256]{1,0:T(8,128)(2,1)} %dy.1) | copy-start | bytes 1572868
  26.3 24.1 %all-to-all-start.1 = ((f32[16,8,128]{2,1,0:T(8,128)}), f32[16,8,128]{2,1,0:T(8,128)S(1)}, u32[]{:S(2)}, u32[]{:S(2)}) async-start(f32[16,8,128]{2,1,0:T(8,128)} %get-tuple-element.13), calls=%async_computation.1 | async-start | bytes 131072 | tf_op jit(solution)/shard_map/all_to_all | solution.py:222
  50.5 16.9 %all-to-all-start = ((bf16[8,256,128]{2,1,0:T(8,128)(2,1)}), bf16[8,256,128]{2,1,0:T(8,128)(2,1)S(1)}, u32[]{:S(2)}, u32[]{:S(2)}) async-start(bf16[8,256,128]{2,1,0:T(8,128)(2,1)} %pack.1), calls=%async_computation | async-start | bytes 1048576 | tf_op jit(solution)/shard_map/all_to_all | solution.py:223

commit v8 on v7

--- a/solution.py
+++ b/solution.py
@@ -17,6 +17,7 @@
 BF16 = jnp.bfloat16
 F32 = jnp.float32
 VMEM = pl.BlockSpec(memory_space=pltpu.VMEM)
+ANY = pl.BlockSpec(memory_space=pl.ANY)
 SMEM = pl.BlockSpec(memory_space=pltpu.SMEM)
 PARAMS = pltpu.CompilerParams(vmem_limit_bytes=24 << 20)
 
@@ -134,9 +135,13 @@
     lax.fori_loop(0, own.shape[0], one_group, 0, unroll=8)
 
 
-def pack_kernel(core, mine, gathered, out):
-    out[:, :LANES, :] = mine[...]
-    out[:, LANES:, :] = gathered[1 - core[0]]
+def pack_kernel(core, mine, gathered, out, sems):
+    first = pltpu.make_async_copy(mine, out.at[:, :LANES, :], sems.at[0])
+    second = pltpu.make_async_copy(gathered.at[1 - core[0]], out.at[:, LANES:, :], sems.at[1])
+    first.start()
+    second.start()
+    first.wait()
+    second.wait()
 
 
 def last_kernel(scale, core, shift, got, parts, wide, narrow):
@@ -155,12 +160,12 @@
         narrow[h * groups : (h + 1) * groups, :] = lags * scale
 
 
-def call(kernel, name, outs, in_specs, scratch=()):
+def call(kernel, name, outs, in_specs, scratch=(), space=VMEM):
     return pl.pallas_call(
         kernel,
         out_shape=outs,
         in_specs=in_specs,
-        out_specs=jax.tree.map(lambda _: VMEM, outs),
+        out_specs=jax.tree.map(lambda _: space, outs),
         scratch_shapes=scratch,
         compiler_params=PARAMS,
         name=name,
@@ -216,7 +221,9 @@
         pack_kernel,
         "pack",
         jax.ShapeDtypeStruct((blocks // 2, 2 * LANES, BLK), BF16),
-        [SMEM] + [VMEM] * 2,
+        [SMEM] + [ANY] * 2,
+        [pltpu.SemaphoreType.DMA((2,))],
+        ANY,
     )(h[None], mine, lax.all_gather(theirs, "core"))
 
     got = lax.all_to_all(send, "z", 0, 0, tiled=True)

time: 68.7 us -> 68.7 us (level)
  no operation moved by 1% of the time
where the time goes in v8:
time: 68.7 us; the launch traced here: 68.4 us
  blocking collectives  25.2 us (37%)
  starting transfers between devices  20.3 us (30%)
  waiting for transfers between devices  11.5 us (17%)
  Pallas kernels  8.27 us (12%)
  local copies, waits for them, and re-layouts  2.09 us (3%)
  between operations  0.77 us (1%)
    all_to_all x1, starting transfers between devices, per_device(): got = lax.all_to_all(send, 'z', 0, 0, tiled=True)  12.6 us
    all_gather x1, blocking collectives, per_device(): parts = lax.all_gather(jnp.sum(got, axis=0), ('xh', 'core'))  11.7 us
    all_gather x2, blocking collectives, swapped(): return lax.all_gather(theirs, 'core')  11 us
    ppermute x2, waiting for transfers between devices, earlier_chip(): return lax.ppermute(block, seq, pairs)  5.99 us
    all_to_all x1, waiting for transfers between devices, per_device(): got = lax.all_to_all(send, 'z', 0, 0, tiled=True)  5.53 us
    all_to_all x1, starting transfers between devices, per_device(): wide = lax.all_to_all(dx, 'grp', 0, 0, tiled=True)  5.21 us
    pallas_call x1, Pallas kernels, per_device(): call(filt_grad_kernel, 'filt_grad', (jax.ShapeDtypeStruct((NOFF, groups,...  3.46 us
    ppermute x2, starting transfers between devices, earlier_chip(): return lax.ppermute(block, seq, pairs)  2.58 us
  transfers between devices with their start and end apart: 4, of which 2 were waited for; matrix products, arithmetic and copies ran while one was open for 1% of the time, Pallas kernels for 6%

profile of v8, /device:TPU:1, one launch (start us, length us, event | category | flops | bytes accessed | tf_op | source)
XLA Modules:
  0.0 68.4 jit_solution(2333061709620217782)
XLA Ops:
  0.6 0.0 copy-start
  0.7 1.1 %constant_dynamic-slice_fusion = (bf16[1024,128]{1,0:T(8,128)(2,1)S(1)}, bf16[1024,128]{1,0:T(8,128)(2,1)S(1)}) fusion(bf16[1024,256]{1,0:T(8,128)(2,1)} %dy.1, s32[]{:T(128)S(6)} %select_n.22, s32[]{:T(128)S(6)} %select_n.21), kind=kLoop, calls=%fused_computation.2 | loop fusion | bytes 1048584 | tf_op jit(solution)/shard_map/dynamic_slice | solution.py:191
  1.8 1.3 %collective-permute-start.1 = (bf16[1024,128]{1,0:T(8,128)(2,1)S(1)}, bf16[1024,128]{1,0:T(8,128)(2,1)S(1)}, u32[]{:S(2)}, u32[]{:S(2)}) collective-permute-start(bf16[1024,128]{1,0:T(8,128)(2,1)S(1)} %get-tuple-element.15), channel_id=1, source_target_pairs={{16,8},{24,0},{32,24},{40,16},{48,40},{56,32},{64,56},{72,48},{80,... | collective-permute-start | bytes 786440 | tf_op jit(solution)/shard_map/ppermute | solution.py:189
  3.1 1.3 %collective-permute-start = (bf16[1024,128]{1,0:T(8,128)(2,1)S(1)}, bf16[1024,128]{1,0:T(8,128)(2,1)S(1)}, u32[]{:S(2)}, u32[]{:S(2)}) collective-permute-start(bf16[1024,128]{1,0:T(8,128)(2,1)S(1)} %get-tuple-element.14), channel_id=1, source_target_pairs={{16,0},{24,8},{32,16},{40,24},{48,32},{56,40},{64,48},{72,56},{80,... | collective-permute-start | bytes 786440 | tf_op jit(solution)/shard_map/ppermute | solution.py:189
  4.4 0.0 copy-start.3
  4.5 0.7 copy-done.3
  5.1 0.1 reduce_sum.18
  5.2 0.1 dynamic-slice.3
  5.3 8.7 %all-gather = bf16[2048,128]{1,0:T(8,128)(2,1)S(1)} all-gather(bf16[1024,128]{1,0:T(8,128)(2,1)S(1)} %get-tuple-element.15), channel_id=2, replica_groups=mesh['z'=16,'xh'=2,'core'=2,'grp'=8] {'core'}, dimensions={0}, use_global_device_ids=true | all-gather | bytes 786432 | tf_op jit(solution)/shard_map/all_gather | solution.py:185
  14.0 2.3 %all-gather.1 = bf16[2048,128]{1,0:T(8,128)(2,1)S(1)} all-gather(bf16[1024,128]{1,0:T(8,128)(2,1)S(1)} %constant_dynamic-slice_fusion.1), channel_id=3, replica_groups=mesh['z'=16,'xh'=2,'core'=2,'grp'=8] {'core'}, dimensions={0}, use_global_device_ids=true | all-gather | bytes 786432 | tf_op jit(solution)/shard_map/all_gather | solution.py:185
  16.3 0.5 own.1
  16.8 0.0 collective-permute-done.1.dy_gathered
  16.8 6.0 %collective-permute-done.dy = bf16[1024,128]{1,0:T(8,128)(2,1)S(1)} collective-permute-done((bf16[1024,128]{1,0:T(8,128)(2,1)S(1)}, bf16[1024,128]{1,0:T(8,128)(2,1)S(1)}, u32[]{:S(2)}, u32[]{:S(2)}) %collective-permute-start) | collective-permute-done | bytes 262176 | tf_op jit(solution)/shard_map/ppermute | solution.py:189
  22.8 0.1 broadcast_in_dim.8.level
  22.9 3.5 %filt_grad.1 = (f32[16,8,128]{2,1,0:T(8,128)}, bf16[8,256,128]{2,1,0:T(8,128)(2,1)S(1)}) custom-call(s32[1]{0:T(128)} %bitcast.core, s32[8,128]{1,0:T(8,128)S(1)} %broadcast_in_dim.8.level, bf16[8,128,256]{2,1,0:T(8,128)(2,1)S(1)} %get-tuple-element.9.x_flip, bf16[8,256,128]{2,1,0:T(8,128)(2,1)S(1)} %get-tuple-element.8.own, ...), custom_call_target="tpu_custom_call" | custom-call | tf_op jit(solution)/shard_map/filt_grad/pallas_call | solution.py:206
  26.3 12.6 %all-to-all-start.1 = ((f32[16,8,128]{2,1,0:T(8,128)}), f32[16,8,128]{2,1,0:T(8,128)S(1)}, u32[]{:S(2)}, u32[]{:S(2)}) async-start(f32[16,8,128]{2,1,0:T(8,128)} %get-tuple-element.13), calls=%async_computation.1 | async-start | bytes 131072 | tf_op jit(solution)/shard_map/all_to_all | solution.py:229
  38.9 0.1 rev.3
  39.0 2.5 %in_grad.1 = (bf16[8,128,128]{2,1,0:T(8,128)(2,1)S(1)}, bf16[8,128,128]{2,1,0:T(8,128)(2,1)S(1)}) custom-call(s32[1]{0:T(128)} %bitcast.core, s32[8,128]{1,0:T(8,128)S(1)} %broadcast_in_dim.8.level, f32[8,16,128]{2,1,0:T(8,128)S(1)} %convert_element_type.3.turned_filt, bf16[8,256,128]{2,1,0:T(8,128)(2,1)S(1)} %get-tuple-element.8.own, ...), custom_call_target="tpu_custom_call" | custom-call | tf_op jit(solution)/shard_map/in_grad/pallas_call | solution.py:214
  41.5 2.6 %all-gather.2 = bf16[16,128,128]{2,1,0:T(8,128)(2,1)S(1)} all-gather(bf16[8,128,128]{2,1,0:T(8,128)(2,1)S(1)} %get-tuple-element.12), channel_id=4, replica_groups=mesh['z'=16,'xh'=2,'core'=2,'grp'=8] {'core'}, dimensions={0}, use_global_device_ids=true | all-gather | bytes 786432 | tf_op jit(solution)/shard_map/all_gather | solution.py:227
  44.1 0.8 %pack.1 = bf16[8,256,128]{2,1,0:T(8,128)(2,1)} custom-call(s32[1]{0:T(128)} %bitcast.core, bf16[8,128,128]{2,1,0:T(8,128)(2,1)S(1)} %get-tuple-element.11.mine, bf16[2,8,128,128]{3,2,1,0:T(8,128)(2,1)S(1)} %bitcast.13), custom_call_target="tpu_custom_call" | custom-call | tf_op jit(solution)/shard_map/pack/pallas_call | solution.py:220
  44.9 5.5 %all-to-all-done.1 = f32[16,8,128]{2,1,0:T(8,128)S(1)} async-done(((f32[16,8,128]{2,1,0:T(8,128)}), f32[16,8,128]{2,1,0:T(8,128)S(1)}, u32[]{:S(2)}, u32[]{:S(2)}) %all-to-all-start.1) | async-done | bytes 65568 | tf_op jit(solution)/shard_map/all_to_all | solution.py:229
  50.5 5.2 %all-to-all-start = ((bf16[8,256,128]{2,1,0:T(8,128)(2,1)}), bf16[8,256,128]{2,1,0:T(8,128)(2,1)S(1)}, u32[]{:S(2)}, u32[]{:S(2)}) async-start(bf16[8,256,128]{2,1,0:T(8,128)(2,1)} %pack.1), calls=%async_computation | async-start | bytes 1048576 | tf_op jit(solution)/shard_map/all_to_all | solution.py:230
  55.7 11.7 %all-gather.3 = f32[32,128]{1,0:T(8,128)S(1)} all-gather(f32[8,128]{1,0:T(8,128)S(1)} %reduce_sum.19), channel_id=5, replica_groups=mesh['z'=16,'xh'=2,'core'=2,'grp'=8] {'xh','core'}, dimensions={0}, use_global_device_ids=true | all-gather | bytes 20480 | tf_op jit(solution)/shard_map/all_gather | solution.py:231
  67.3 1.0 %last.1 = (bf16[128,2048]{1,0:T(8,128)(2,1)}, f32[16,32]{1,0:T(8,128)}) custom-call(s32[1]{0:T(128)} %bitcast.core, s32[1]{0:T(128)} %bitcast.1.shift, bf16[8,256,128]{2,1,0:T(8,128)(2,1)S(1)} %all-to-all-done.got, f32[4,8,128]{2,1,0:T(8,128)S(1)} %bitcast.14), custom_call_target="tpu_custom_call" | custom-call | tf_op jit(solution)/shard_map/last/pallas_call | solution.py:234
  (11 shorter events, 0.1 us)
Async XLA Ops:
  0.6 38.3 %copy-start = (bf16[16,2048]{1,0:T(8,128)(2,1)S(1)}, bf16[16,2048]{1,0:T(8,128)(2,1)}, u32[]{:S(2)}) copy-start(bf16[16,2048]{1,0:T(8,128)(2,1)} %param.6) | copy-start | bytes 196612
  0.7 3.7 %copy-start.2 = (bf16[1024,256]{1,0:T(8,128)(2,1)S(1)}, bf16[1024,256]{1,0:T(8,128)(2,1)}, u32[]{:S(2)}) copy-start(bf16[1024,256]{1,0:T(8,128)(2,1)} %x.1) | copy-start | bytes 1572868
  1.8 15.0 %collective-permute-start.1 = (bf16[1024,128]{1,0:T(8,128)(2,1)S(1)}, bf16[1024,128]{1,0:T(8,128)(2,1)S(1)}, u32[]{:S(2)}, u32[]{:S(2)}) collective-permute-start(bf16[1024,128]{1,0:T(8,128)(2,1)S(1)} %get-tuple-element.15), channel_id=1, source_target_pairs={{16,8},{24,0},{32,24},{40,16},{48,40},{56,32},{64,56},{72,48},{80,... | collective-permute-start | bytes 786440 | tf_op jit(solution)/shard_map/ppermute | solution.py:189
  3.1 19.7 %collective-permute-start = (bf16[1024,128]{1,0:T(8,128)(2,1)S(1)}, bf16[1024,128]{1,0:T(8,128)(2,1)S(1)}, u32[]{:S(2)}, u32[]{:S(2)}) collective-permute-start(bf16[1024,128]{1,0:T(8,128)(2,1)S(1)} %get-tuple-element.14), channel_id=1, source_target_pairs={{16,0},{24,8},{32,16},{40,24},{48,32},{56,40},{64,48},{72,56},{80,... | collective-permute-start | bytes 786440 | tf_op jit(solution)/shard_map/ppermute | solution.py:189
  4.4 0.7 %copy-start.3 = (s32[16,16]{1,0:T(8,128)S(1)}, s32[16,16]{1,0:T(8,128)}, u32[]{:S(2)}) copy-start(s32[16,16]{1,0:T(8,128)} %param.7) | copy-start | bytes 3076
  14.0 2.3 %copy-start.1 = (bf16[1024,256]{1,0:T(8,128)(2,1)S(1)}, bf16[1024,256]{1,0:T(8,128)(2,1)}, u32[]{:S(2)}) copy-start(bf16[1024,256]{1,0:T(8,128)(2,1)} %dy.1) | copy-start | bytes 1572868
  26.3 24.1 %all-to-all-start.1 = ((f32[16,8,128]{2,1,0:T(8,128)}), f32[16,8,128]{2,1,0:T(8,128)S(1)}, u32[]{:S(2)}, u32[]{:S(2)}) async-start(f32[16,8,128]{2,1,0:T(8,128)} %get-tuple-element.13), calls=%async_computation.1 | async-start | bytes 131072 | tf_op jit(solution)/shard_map/all_to_all | solution.py:229
  50.5 16.9 %all-to-all-start = ((bf16[8,256,128]{2,1,0:T(8,128)(2,1)}), bf16[8,256,128]{2,1,0:T(8,128)(2,1)S(1)}, u32[]{:S(2)}, u32[]{:S(2)}) async-start(bf16[8,256,128]{2,1,0:T(8,128)(2,1)} %pack.1), calls=%async_computation | async-start | bytes 1048576 | tf_op jit(solution)/shard_map/all_to_all | solution.py:230

commit v9 on v7

--- a/solution.py
+++ b/solution.py
@@ -183,7 +183,8 @@
         pairs = [(i, (i ^ swap) - 2) for i in range(2, 2 * chips)]
         return lax.ppermute(block, seq, pairs)
 
-    later_same = earlier_chip(lax.dynamic_slice_in_dim(out_grad, h * LANES, LANES, 1), 0)
+    dy_mine = lax.dynamic_slice_in_dim(out_grad, h * LANES, LANES, 1)
+    later_same = earlier_chip(dy_mine, 0)
     later_other = earlier_chip(lax.dynamic_slice_in_dim(out_grad, (1 - h) * LANES, LANES, 1), 1)
 
     level = lax.dynamic_slice_in_dim(jnp.sum(band, axis=1, keepdims=True), h * groups, groups, 0)
@@ -197,7 +198,7 @@
         (turned_shape, jax.ShapeDtypeStruct((groups, BLK, blocks * CPG), BF16)),
         [SMEM] + [VMEM] * 4,
         [pltpu.VMEM(turned_shape.shape, BF16)],
-    )(h[None], out_grad, swapped(out_grad), inputs, swapped(inputs))
+    )(h[None], dy_mine, swapped(out_grad), inputs, swapped(inputs))
     send, later = call(
         filt_grad_kernel,
         "filt_grad",

time: 68.7 us -> 68.5 us (level)
  starting transfers between devices: 20.3 us -> 19 us
  waiting for transfers between devices: 11.5 us -> 12.5 us
    all_to_all x1, starting transfers between devices: 12.6 us -> 11.2 us  [per_device(): got = lax.all_to_all(send, 'z', 0, 0, tiled=True)]
    dynamic_slice x1 -> x0, local copies, waits for them, and re-layouts: 1.13 us -> none  [per_device(): lax.dynamic_slice_in_dim(out_grad, h * LANES, LANES, 1)]
    dynamic_slice x1 -> x2, local copies, waits for them, and re-layouts: 0.03 us -> 1.16 us  [swapped(): theirs = lax.dynamic_slice_in_dim(whole, (1 - h) * LANES, LANES, 1)]
    ppermute x2, waiting for transfers between devices: 5.99 us -> 6.71 us  [earlier_chip(): return lax.ppermute(block, seq, pairs)]
where the time goes in v9:
time: 68.5 us; the launch traced here: 68.1 us
  blocking collectives  25.4 us (37%)
  starting transfers between devices  19 us (28%)
  waiting for transfers between devices  12.5 us (18%)
  Pallas kernels  8.26 us (12%)
  local copies, waits for them, and re-layouts  2.09 us (3%)
  between operations  0.76 us (1%)
    all_gather x1, blocking collectives, per_device(): parts = lax.all_gather(jnp.sum(got, axis=0), ('xh', 'core'))  12.1 us
    all_to_all x1, starting transfers between devices, per_device(): got = lax.all_to_all(send, 'z', 0, 0, tiled=True)  11.2 us
    all_gather x2, blocking collectives, swapped(): return lax.all_gather(theirs, 'core')  10.8 us
    ppermute x2, waiting for transfers between devices, earlier_chip(): return lax.ppermute(block, seq, pairs)  6.71 us
    all_to_all x1, waiting for transfers between devices, per_device(): got = lax.all_to_all(send, 'z', 0, 0, tiled=True)  5.77 us
    all_to_all x1, starting transfers between devices, per_device(): wide = lax.all_to_all(dx, 'grp', 0, 0, tiled=True)  5.23 us
    pallas_call x1, Pallas kernels, per_device(): call(filt_grad_kernel, 'filt_grad', (jax.ShapeDtypeStruct((NOFF, groups,...  3.44 us
    ppermute x2, starting transfers between devices, earlier_chip(): return lax.ppermute(block, seq, pairs)  2.58 us
  transfers between devices with their start and end apart: 4, of which 2 were waited for; matrix products, arithmetic and copies ran while one was open for 1% of the time, Pallas kernels for 6%

profile of v9, /device:TPU:1, one launch (start us, length us, event | category | flops | bytes accessed | tf_op | source)
XLA Modules:
  0.0 68.1 jit_solution(11786204483156617813)
XLA Ops:
  0.6 0.0 copy-start
  0.7 1.1 %constant_dynamic-slice_fusion.1 = (bf16[1024,128]{1,0:T(8,128)(2,1)S(1)}, bf16[1024,128]{1,0:T(8,128)(2,1)S(1)}) fusion(bf16[1024,256]{1,0:T(8,128)(2,1)} %param.5, s32[]{:T(128)S(6)} %select_n.22, s32[]{:T(128)S(6)} %select_n.21), kind=kLoop, calls=%fused_computation.3 | loop fusion | bytes 1048584 | tf_op jit(solution)/shard_map/dynamic_slice | solution.py:179
  1.8 1.3 %collective-permute-start = (bf16[1024,128]{1,0:T(8,128)(2,1)S(1)}, bf16[1024,128]{1,0:T(8,128)(2,1)S(1)}, u32[]{:S(2)}, u32[]{:S(2)}) collective-permute-start(bf16[1024,128]{1,0:T(8,128)(2,1)S(1)} %get-tuple-element.15.dy), channel_id=1, source_target_pairs={{16,0},{24,8},{32,16},{40,24},{48,32},{56,40},{64,48},{72,56},{80,... | collective-permute-start | bytes 786440 | tf_op jit(solution)/shard_map/ppermute | solution.py:184
  3.1 1.3 %collective-permute-start.1 = (bf16[1024,128]{1,0:T(8,128)(2,1)S(1)}, bf16[1024,128]{1,0:T(8,128)(2,1)S(1)}, u32[]{:S(2)}, u32[]{:S(2)}) collective-permute-start(bf16[1024,128]{1,0:T(8,128)(2,1)S(1)} %get-tuple-element.14), channel_id=1, source_target_pairs={{16,8},{24,0},{32,24},{40,16},{48,40},{56,32},{64,56},{72,48},{80,... | collective-permute-start | bytes 786440 | tf_op jit(solution)/shard_map/ppermute | solution.py:184
  4.4 0.0 copy-start.2
  4.5 0.7 copy-done.2
  5.1 0.1 reduce_sum.18
  5.2 0.1 dynamic-slice.3
  5.3 8.7 %all-gather = bf16[2048,128]{1,0:T(8,128)(2,1)S(1)} all-gather(bf16[1024,128]{1,0:T(8,128)(2,1)S(1)} %get-tuple-element.14), channel_id=2, replica_groups=mesh['z'=16,'xh'=2,'core'=2,'grp'=8] {'core'}, dimensions={0}, use_global_device_ids=true | all-gather | bytes 786432 | tf_op jit(solution)/shard_map/all_gather | solution.py:180
  14.0 2.2 %all-gather.1 = bf16[2048,128]{1,0:T(8,128)(2,1)S(1)} all-gather(bf16[1024,128]{1,0:T(8,128)(2,1)S(1)} %constant_dynamic-slice_fusion), channel_id=3, replica_groups=mesh['z'=16,'xh'=2,'core'=2,'grp'=8] {'core'}, dimensions={0}, use_global_device_ids=true | all-gather | bytes 786432 | tf_op jit(solution)/shard_map/all_gather | solution.py:180
  16.1 0.5 own.1
  16.7 0.0 collective-permute-done.dy
  16.7 6.7 %collective-permute-done.1.dy_gathered = bf16[1024,128]{1,0:T(8,128)(2,1)S(1)} collective-permute-done((bf16[1024,128]{1,0:T(8,128)(2,1)S(1)}, bf16[1024,128]{1,0:T(8,128)(2,1)S(1)}, u32[]{:S(2)}, u32[]{:S(2)}) %collective-permute-start.1) | collective-permute-done | bytes 262176 | tf_op jit(solution)/shard_map/ppermute | solution.py:184
  23.4 0.1 broadcast_in_dim.8.level
  23.4 3.4 %filt_grad.1 = (f32[16,8,128]{2,1,0:T(8,128)}, bf16[8,256,128]{2,1,0:T(8,128)(2,1)S(1)}) custom-call(s32[1]{0:T(128)} %bitcast.core, s32[8,128]{1,0:T(8,128)S(1)} %broadcast_in_dim.8.level, bf16[8,128,256]{2,1,0:T(8,128)(2,1)S(1)} %get-tuple-element.9.x_flip, bf16[8,256,128]{2,1,0:T(8,128)(2,1)S(1)} %get-tuple-element.8.own, ...), custom_call_target="tpu_custom_call" | custom-call | tf_op jit(solution)/shard_map/filt_grad/pallas_call | solution.py:202
  26.9 11.2 %all-to-all-start.1 = ((f32[16,8,128]{2,1,0:T(8,128)}), f32[16,8,128]{2,1,0:T(8,128)S(1)}, u32[]{:S(2)}, u32[]{:S(2)}) async-start(f32[16,8,128]{2,1,0:T(8,128)} %get-tuple-element.13), calls=%async_computation.1 | async-start | bytes 131072 | tf_op jit(solution)/shard_map/all_to_all | solution.py:223
  38.2 0.1 rev.3
  38.3 2.5 %in_grad.1 = (bf16[8,128,128]{2,1,0:T(8,128)(2,1)S(1)}, bf16[8,128,128]{2,1,0:T(8,128)(2,1)S(1)}) custom-call(s32[1]{0:T(128)} %bitcast.core, s32[8,128]{1,0:T(8,128)S(1)} %broadcast_in_dim.8.level, f32[8,16,128]{2,1,0:T(8,128)S(1)} %convert_element_type.3.turned_filt, bf16[8,256,128]{2,1,0:T(8,128)(2,1)S(1)} %get-tuple-element.8.own, ...), custom_call_target="tpu_custom_call" | custom-call | tf_op jit(solution)/shard_map/in_grad/pallas_call | solution.py:210
  40.8 2.4 %all-gather.2 = bf16[16,128,128]{2,1,0:T(8,128)(2,1)S(1)} all-gather(bf16[8,128,128]{2,1,0:T(8,128)(2,1)S(1)} %get-tuple-element.12), channel_id=4, replica_groups=mesh['z'=16,'xh'=2,'core'=2,'grp'=8] {'core'}, dimensions={0}, use_global_device_ids=true | all-gather | bytes 786432 | tf_op jit(solution)/shard_map/all_gather | solution.py:221
  43.2 0.8 %pack.1 = bf16[8,256,128]{2,1,0:T(8,128)(2,1)} custom-call(s32[1]{0:T(128)} %bitcast.core, bf16[8,128,128]{2,1,0:T(8,128)(2,1)S(1)} %get-tuple-element.11.mine, bf16[2,8,128,128]{3,2,1,0:T(8,128)(2,1)S(1)} %bitcast.11), custom_call_target="tpu_custom_call" | custom-call | tf_op jit(solution)/shard_map/pack/pallas_call | solution.py:216
  44.0 5.8 %all-to-all-done.1 = f32[16,8,128]{2,1,0:T(8,128)S(1)} async-done(((f32[16,8,128]{2,1,0:T(8,128)}), f32[16,8,128]{2,1,0:T(8,128)S(1)}, u32[]{:S(2)}, u32[]{:S(2)}) %all-to-all-start.1) | async-done | bytes 65568 | tf_op jit(solution)/shard_map/all_to_all | solution.py:223
  49.7 5.2 %all-to-all-start = ((bf16[8,256,128]{2,1,0:T(8,128)(2,1)}), bf16[8,256,128]{2,1,0:T(8,128)(2,1)S(1)}, u32[]{:S(2)}, u32[]{:S(2)}) async-start(bf16[8,256,128]{2,1,0:T(8,128)(2,1)} %pack.1), calls=%async_computation | async-start | bytes 1048576 | tf_op jit(solution)/shard_map/all_to_all | solution.py:224
  55.0 12.1 %all-gather.3 = f32[32,128]{1,0:T(8,128)S(1)} all-gather(f32[8,128]{1,0:T(8,128)S(1)} %reduce_sum.19), channel_id=5, replica_groups=mesh['z'=16,'xh'=2,'core'=2,'grp'=8] {'xh','core'}, dimensions={0}, use_global_device_ids=true | all-gather | bytes 20480 | tf_op jit(solution)/shard_map/all_gather | solution.py:225
  67.1 1.0 %last.1 = (bf16[128,2048]{1,0:T(8,128)(2,1)}, f32[16,32]{1,0:T(8,128)}) custom-call(s32[1]{0:T(128)} %bitcast.core, s32[1]{0:T(128)} %bitcast.1.shift, bf16[8,256,128]{2,1,0:T(8,128)(2,1)S(1)} %all-to-all-done.got, f32[4,8,128]{2,1,0:T(8,128)S(1)} %bitcast.14), custom_call_target="tpu_custom_call" | custom-call | tf_op jit(solution)/shard_map/last/pallas_call | solution.py:228
  (9 shorter events, 0.1 us)
Async XLA Ops:
  0.6 37.5 %copy-start = (bf16[16,2048]{1,0:T(8,128)(2,1)S(1)}, bf16[16,2048]{1,0:T(8,128)(2,1)}, u32[]{:S(2)}) copy-start(bf16[16,2048]{1,0:T(8,128)(2,1)} %param.6) | copy-start | bytes 196612
  0.7 3.7 %copy-start.1 = (bf16[1024,256]{1,0:T(8,128)(2,1)S(1)}, bf16[1024,256]{1,0:T(8,128)(2,1)}, u32[]{:S(2)}) copy-start(bf16[1024,256]{1,0:T(8,128)(2,1)} %x.1) | copy-start | bytes 1572868
  1.8 14.9 %collective-permute-start = (bf16[1024,128]{1,0:T(8,128)(2,1)S(1)}, bf16[1024,128]{1,0:T(8,128)(2,1)S(1)}, u32[]{:S(2)}, u32[]{:S(2)}) collective-permute-start(bf16[1024,128]{1,0:T(8,128)(2,1)S(1)} %get-tuple-element.15.dy), channel_id=1, source_target_pairs={{16,0},{24,8},{32,16},{40,24},{48,32},{56,40},{64,48},{72,56},{80,... | collective-permute-start | bytes 786440 | tf_op jit(solution)/shard_map/ppermute | solution.py:184
  3.1 20.3 %collective-permute-start.1 = (bf16[1024,128]{1,0:T(8,128)(2,1)S(1)}, bf16[1024,128]{1,0:T(8,128)(2,1)S(1)}, u32[]{:S(2)}, u32[]{:S(2)}) collective-permute-start(bf16[1024,128]{1,0:T(8,128)(2,1)S(1)} %get-tuple-element.14), channel_id=1, source_target_pairs={{16,8},{24,0},{32,24},{40,16},{48,40},{56,32},{64,56},{72,48},{80,... | collective-permute-start | bytes 786440 | tf_op jit(solution)/shard_map/ppermute | solution.py:184
  4.4 0.7 %copy-start.2 = (s32[16,16]{1,0:T(8,128)S(1)}, s32[16,16]{1,0:T(8,128)}, u32[]{:S(2)}) copy-start(s32[16,16]{1,0:T(8,128)} %param.7) | copy-start | bytes 3076
  26.9 22.9 %all-to-all-start.1 = ((f32[16,8,128]{2,1,0:T(8,128)}), f32[16,8,128]{2,1,0:T(8,128)S(1)}, u32[]{:S(2)}, u32[]{:S(2)}) async-start(f32[16,8,128]{2,1,0:T(8,128)} %get-tuple-element.13), calls=%async_computation.1 | async-start | bytes 131072 | tf_op jit(solution)/shard_map/all_to_all | solution.py:223
  49.7 17.4 %all-to-all-start = ((bf16[8,256,128]{2,1,0:T(8,128)(2,1)}), bf16[8,256,128]{2,1,0:T(8,128)(2,1)S(1)}, u32[]{:S(2)}, u32[]{:S(2)}) async-start(bf16[8,256,128]{2,1,0:T(8,128)(2,1)} %pack.1), calls=%async_computation | async-start | bytes 1048576 | tf_op jit(solution)/shard_map/all_to_all | solution.py:224
